TPU v7x, 128 devices: a whole 4x4x4 slice. The times are simulated.
128 devices in a mesh: box: 8 (over z, y_lo), dir: 16 (over y_hi, x, core).
Axes of the slice: x: 4, y: 4 (y_hi: 2, y_lo: 2; y = y_hi * 2 + y_lo), z: 4, core: 2. Of those that a mesh axis runs over, the one named last changes fastest.
Arguments:
- child_rad: float32 [800, 16, 2, 2, 384], P('dir', 'box'), may hold values from -6 to 6
- box_at_slot: int32 [8], replicated, may hold values from 0 to 7, each once
- octant: int32 [16], replicated, may hold values from 0 to 7, as said below
- far_par: int32 [8, 3], replicated, may hold values from 0 to 7, as said below
- far_par_off: int32 [8, 3], replicated, may hold values from 0 to 7
- far_child: int32 [16, 7], replicated, may hold values from 0 to 15, as said below
- far_child_off: int32 [16, 7], replicated, may hold values from 0 to 15
- far_child_count: int32 [16], replicated, may hold values from 2 to 7
- trans_par: float32 [1600, 8, 2, 768], P('dir'), may hold values from -1.8 to 1.8
- trans_child: float32 [800, 16, 2, 384], P('dir'), may hold values from -1.8 to 1.8
Outputs:
- child_in: float32 [800, 16, 2, 2, 384], P('dir', 'box')
Inputs may be any that keep to these rules, and one draw needn't show every extreme that they name: `box_at_slot`: a permutation of the parent boxes. `octant`: the children of one parent box lie in different octants. `far_par`: row b lists 3 different parent boxes, none of them b. `far_child`: row c lists 7 different child boxes, none of them c; only the first far_child_count[c] entries are used.
All inputs are finite; a program needn't handle non-finite values.
Results may differ from a plain program's by a relative error of at most 0.00018.
Values sent between devices are 32-bit elements; how exact they have to be, the bound alone decides.
A program may use at most 128 MiB of HBM per device.

v0:
```python
import math

import jax
import jax.numpy as jnp
from jax import lax
from jax.sharding import PartitionSpec as P

KIDS = 2


offset_phase = 32.0 * math.pi
highest = lax.Precision.HIGHEST


def theta_table(child_count):
    parent_rows = jnp.arange(2 * child_count, dtype=jnp.int32)
    lowest = (parent_rows - 1) // 2
    first_node = jnp.clip(lowest - 2, 0, child_count - 6)
    offset = parent_rows.astype(jnp.float32) * 0.5 - 0.25 - first_node.astype(jnp.float32)
    columns = jnp.arange(child_count, dtype=jnp.int32)
    lagrange = jnp.zeros((2 * child_count, child_count), jnp.float32)
    for node_index in range(6):
        weight = jnp.ones_like(offset)
        for other_node in range(6):
            if other_node != node_index:
                weight = weight * (offset - float(other_node)) / float(node_index - other_node)
        match_mask = (columns[None, :] == (first_node + node_index)[:, None]).astype(jnp.float32)
        lagrange = lagrange + weight[:, None] * match_mask
    return lagrange


def phi_kernel(parent_index, child_index, child_count):
    period = 4 * child_count
    parity_odd = 2 * parent_index - 4 * child_index - 1
    numerator = jnp.mod((child_count - 1) * parity_odd, 2 * period).astype(jnp.float32)
    denominator = parity_odd.astype(jnp.float32)
    return jnp.sin(math.pi * numerator / period) / (
        child_count * jnp.sin(math.pi * denominator / period)
    )


def directions(phi_index, phi_count, theta_count):
    theta_angle = (jnp.arange(theta_count, dtype=jnp.int32).astype(jnp.float32) + 0.5) * (
        math.pi / theta_count
    )
    phi_angle = (phi_index.astype(jnp.float32) + 0.5) * (2.0 * math.pi / phi_count)
    sin_theta = jnp.sin(theta_angle)[None, :]
    east_part = sin_theta * jnp.cos(phi_angle)[:, None]
    north_part = sin_theta * jnp.sin(phi_angle)[:, None]
    upward = jnp.broadcast_to(jnp.cos(theta_angle)[None, :], east_part.shape)
    return (east_part, north_part, upward)


def rotate(pattern, octants, east_part, north_part, upward, phase_sign):
    sign_east = (jnp.mod(octants, 2) * 2 - 1).astype(jnp.float32)
    sign_north = (jnp.mod(octants // 2, 2) * 2 - 1).astype(jnp.float32)
    sign_up = (jnp.mod(octants // 4, 2) * 2 - 1).astype(jnp.float32)
    angle_all = offset_phase * (
        sign_east[None, :, None] * east_part[:, None, :]
        + sign_north[None, :, None] * north_part[:, None, :]
        + sign_up[None, :, None] * upward[:, None, :]
    )
    cosine = jnp.cos(angle_all)[:, :, None, :]
    sine_part = phase_sign * jnp.sin(angle_all)[:, :, None, :]
    real_part = pattern[:, :, 0]
    imag_part = pattern[:, :, 1]
    return jnp.stack(
        [cosine * real_part - sine_part * imag_part, sine_part * real_part + cosine * imag_part],
        axis=2,
    )


def complex_mul(translation, pattern):
    table_real = translation[:, :, 0][:, :, None, :]
    table_imag = translation[:, :, 1][:, :, None, :]
    field_real = pattern[:, :, 0]
    field_imag = pattern[:, :, 1]
    return jnp.stack(
        [
            table_real * field_real - table_imag * field_imag,
            table_real * field_imag + table_imag * field_real,
        ],
        axis=2,
    )


def shards(
    child_rad,
    box_at_slot,
    octant,
    far_par,
    far_par_off,
    far_child,
    far_child_off,
    far_child_count,
    trans_par,
    trans_child,
):
    child_rows = child_rad.shape[0]
    kid_count = child_rad.shape[1]
    theta_child = child_rad.shape[4]
    dir_count = lax.axis_size("dir")
    parent_rows = 2 * child_rows
    child_total = child_rows * dir_count
    parent_total = 2 * child_total
    parents_here = kid_count // KIDS
    box_index = lax.axis_index("box")
    dir_index = lax.axis_index("dir")
    theta_map = theta_table(theta_child)
    parent_phi = dir_index * parent_rows + jnp.arange(parent_rows, dtype=jnp.int32)
    child_phi = dir_index * child_rows + jnp.arange(child_rows, dtype=jnp.int32)
    east_part, north_part, upward = directions(parent_phi, parent_total, 2 * theta_child)
    slot_lookup = jnp.argsort(box_at_slot)
    own_boxes = lax.dynamic_slice_in_dim(box_at_slot, box_index * parents_here, parents_here)
    kid_boxes = (own_boxes[:, None] * KIDS + jnp.arange(KIDS, dtype=jnp.int32)[None, :]).reshape(-1)
    kid_octants = jnp.take(octant, kid_boxes)
    shard_piece = lax.all_gather(child_rad, "dir", axis=0, tiled=True)
    columns = jnp.arange(shard_piece.shape[0], dtype=jnp.int32)
    kernel = phi_kernel(parent_phi[:, None], columns[None, :], child_total)
    spread = jnp.einsum("pc,cnabt->pnabt", kernel, shard_piece, precision=highest)
    widened = jnp.einsum("pnabt,qt->pnabq", spread, theta_map, precision=highest)
    shifted = rotate(widened, kid_octants, east_part, north_part, upward, 1.0)
    parent_rad = shifted.reshape(parent_rows, parents_here, KIDS, 2, 2, 2 * theta_child).sum(axis=2)
    parent_from = jnp.take(slot_lookup, jnp.take(far_par, own_boxes, axis=0))
    parent_offsets = jnp.take(far_par_off, own_boxes, axis=0)
    running_sum = jnp.zeros_like(parent_rad)
    shard_piece = lax.all_gather(parent_rad, "box", axis=1, tiled=True)
    first_row = jnp.int32(0)
    width_here = shard_piece.shape[1]
    for far_slot in range(parent_from.shape[1]):
        source = parent_from[:, far_slot]
        inside = (source >= first_row) & (source < first_row + width_here)
        local_index = jnp.clip(source, 0, width_here - 1)
        picked = jnp.take(shard_piece, local_index, axis=1)
        tables = jnp.take(trans_par, parent_offsets[:, far_slot], axis=1)
        running_sum = running_sum + jnp.where(
            inside[None, :, None, None, None], complex_mul(tables, picked), 0.0
        )
    returned = rotate(
        jnp.repeat(running_sum, KIDS, axis=1), kid_octants, east_part, north_part, upward, -1.0
    )
    narrowed = 0.5 * jnp.einsum("pnabq,qt->pnabt", returned, theta_map, precision=highest)
    shard_piece = lax.all_gather(narrowed, "dir", axis=0, tiled=True)
    parent_cols = jnp.arange(shard_piece.shape[0], dtype=jnp.int32)
    kernel = phi_kernel(parent_cols[None, :], child_phi[:, None], child_total)
    descended = 0.5 * jnp.einsum("cp,pnabt->cnabt", kernel, shard_piece, precision=highest)
    source_ids = jnp.take(far_child, kid_boxes, axis=0)
    kid_sources = jnp.take(slot_lookup, source_ids // KIDS) * KIDS + source_ids % KIDS
    kid_offsets = jnp.take(far_child_off, kid_boxes, axis=0)
    kid_lengths = jnp.take(far_child_count, kid_boxes)
    longest = jnp.max(kid_lengths)
    shard_piece = lax.all_gather(child_rad, "box", axis=1, tiled=True)
    first_row = jnp.int32(0)
    width_here = shard_piece.shape[1]

    def one_entry(far_slot, partial_sum):
        source = lax.dynamic_index_in_dim(kid_sources, far_slot, 1, keepdims=False)
        offsets = lax.dynamic_index_in_dim(kid_offsets, far_slot, 1, keepdims=False)
        active = (
            (far_slot < kid_lengths) & (source >= first_row) & (source < first_row + width_here)
        )
        local_index = jnp.clip(source, 0, width_here - 1)
        picked = jnp.take(shard_piece, local_index, axis=1)
        tables = jnp.take(trans_child, offsets, axis=1)
        return partial_sum + jnp.where(
            active[None, :, None, None, None], complex_mul(tables, picked), 0.0
        )

    child_far = lax.fori_loop(0, longest, one_entry, jnp.zeros_like(child_rad))
    return descended + child_far


def solution(mesh):
    return jax.shard_map(
        shards,
        mesh=mesh,
        in_specs=(
            P("dir", "box", None, None, None),
            P(),
            P(),
            P(),
            P(),
            P(),
            P(),
            P(),
            P("dir", None, None, None),
            P("dir", None, None, None),
        ),
        out_specs=P("dir", "box", None, None, None),
        check_vma=False,
    )
```

profile of v0, /device:TPU:1, one launch (start us, length us, event | category | flops | bytes accessed | tf_op | source)
XLA Modules:
  0.0 585.4 jit_solution(15059608070569397302)
XLA Ops:
  6.5 0.7 all-gather.6.cloned.1.call-update
  7.3 1.2 dynamic_slice.10
  9.2 0.6 gather_fusion.4
  10.3 2.4 broadcast_multiply_fusion
  12.7 79.4 %all-gather.6.cloned.1.call-done = f32[800,2,2,2,384]{4,3,2,1,0:T(2,128)} async-done(((f32[50,2,2,2,384]{4,3,2,1,0:T(2,128)}), f32[800,2,2,2,384]{4,3,2,1,0:T(2,128)}) %all-gather.6.cloned.1.call-update) | async-done | bytes 9830416 | tf_op jit(solution)/shard_map/all_gather | solution.py:117
  92.2 25.4 %fusion.3 = f32[100,2,2,2,384]{4,0,3,2,1:T(8,128)S(1)} fusion(f32[800,2,2,2,384]{4,3,2,1,0:T(2,128)} %all-gather.6.cloned.1.call-done, s32[800]{0:T(1024)S(1)} %iota_multiply_fusion.1, s32[100]{0:T(128)S(1)} %fusion.117), kind=kOutput, calls=%fused_computation.27 | convolution fusion | flops 2950320128 | bytes 11062800 | tf_op jit(solution)/shard_map/pc,cnabt->pnabt/dot_general | solution.py:120
  117.6 7.3 %fusion.21 = f32[100,2,2,2,768]{4,0,3,2,1:T(8,128)S(1)} fusion(f32[100,2,2,2,384]{4,0,3,2,1:T(8,128)S(1)} %fusion.3, f32[768]{0:T(1024)S(1)} %get-tuple-element.198, s32[768]{0:T(1024)S(1)} %get-tuple-element.201, f32[768]{0:T(1024)S(1)} %get-tuple-element.197, s32[768]{0:T(1024)S(1)} %get-tuple-element.202, f32[768]{0:T(1024)S(1)} %get-tuple-element.196, ...), kind=kOutput, calls=%fused_computation.56 | convolution fusion | flops 2836168704 | bytes 3723264 | tf_op jit(solution)/shard_map/pnabt,qt->pnabq/dot_general | solution.py:121
  124.9 0.3 multiply_subtract_fusion.2
  125.4 1.7 copy.61
  127.1 0.7 all-gather.10.cloned.1.call-update
  129.9 0.6 fusion.137
  136.1 1.0 sort.17
  137.2 0.6 gather_fusion.2
  137.8 0.6 fusion.138
  144.2 2.1 constant_dynamic-slice_fusion.1
  146.7 173.4 %all-gather.12.cloned.1.call-done = f32[100,16,2,768]{3,2,0,1:T(2,128)} async-done(((f32[100,2,2,768]{3,2,0,1:T(2,128)}), f32[100,16,2,768]{3,2,0,1:T(2,128)}) %all-gather.12.cloned.1.call-update) | async-done | bytes 9830416 | tf_op jit(solution)/shard_map/all_gather | solution.py:127
  320.1 3.3 constant_dynamic-slice_fusion.7
  324.3 0.3 fusion.13
  324.7 0.3 multiply_subtract_fusion.1
  325.0 5.1 fusion.9
  330.1 1.8 copy.67
  331.9 0.6 gather_fusion.5
  332.6 0.6 gather_fusion.6
  333.3 0.6 gather_fusion.7
  334.1 0.7 gather_fusion.3
  335.0 0.7 fusion.134
  335.7 91.0 %all-gather.10.cloned.1.call-done = f32[50,16,2,2,384]{4,3,2,1,0:T(2,128)} async-done(((f32[50,2,2,2,384]{4,3,2,1,0:T(2,128)}), f32[50,16,2,2,384]{4,3,2,1,0:T(2,128)}) %all-gather.10.cloned.1.call-update) | async-done | bytes 4915216 | tf_op jit(solution)/shard_map/all_gather | solution.py:152
  426.9 28.1 %while.13 = (s32[]{:T(128)}, f32[50,2,2,2,384]{4,3,2,0,1:T(2,128)S(1)}, s32[]{:T(128)}, s32[2]{0:T(128)S(1)}, s32[2,7]{0,1:T(8,128)S(1)}, /*index=5*/s32[2,7]{0,...) while((s32[]{:T(128)}, ...), condition=%wide.region_4.10_spmd, body=%wide.region_3.9_spmd.sunk | while | flops 1154089 | bytes 8917247 | solution.py:169
  427.6 2.6 gather_fusion.1
  430.5 0.2 fusion.142
  430.9 3.7 gather_fusion
  434.6 0.3 select_bitcast_fusion.4
  434.9 0.3 multiply_subtract_fusion.4
  435.3 0.6 fusion.143
  436.5 2.6 gather_fusion.1
  439.8 4.2 gather_fusion
  444.0 0.3 select_bitcast_fusion.4
  444.4 0.3 multiply_subtract_fusion.4
  444.7 0.6 fusion.143
  446.0 2.7 gather_fusion.1
  448.8 0.2 fusion.142
  449.3 3.7 gather_fusion
  453.0 0.3 select_bitcast_fusion.4
  453.3 0.3 multiply_subtract_fusion.4
  453.7 0.6 fusion.143
  455.0 98.3 %all-gather.8.cloned.1.call-done = f32[1600,2,2,2,384]{4,3,2,1,0:T(2,128)} async-done(((f32[100,2,2,2,384]{4,3,2,1,0:T(2,128)}), f32[1600,2,2,2,384]{4,3,2,1,0:T(2,128)}) %all-gather.8.cloned.1.call-update) | async-done | bytes 19660816 | tf_op jit(solution)/shard_map/all_gather | solution.py:143
  553.3 24.0 %fusion.17 = f32[50,2,2,2,384]{4,0,3,2,1:T(8,128)S(1)} fusion(f32[1600,2,2,2,384]{4,3,2,1,0:T(2,128)} %all-gather.8.cloned.1.call-done, f32[50,2,2,2,384]{4,3,2,0,1:T(2,128)S(1)} %get-tuple-element.55, s32[50]{0:T(128)S(1)} %add_multiply_fusion.8, s32[1600]{0:T(1024)S(1)} %iota_multiply_fusion), kind=kOutput, calls=%fused_computation.54 | convolution fusion | flops 2950627328 | bytes 20896200 | tf_op jit(solution)/shard_map/cp,pnabt->cnabt/dot_general | solution.py:146
  577.3 1.1 copy.74
  (99 shorter events, 4.7 us)
Async XLA Ops:
  6.5 2.7 copy-start
  6.5 85.6 %all-gather.6.cloned.1.call-start = ((), (), s32[]{:S(2)}) async-start(), calls=%async_computation | async-start | bytes 10444800 | tf_op jit(solution)/shard_map/all_gather | solution.py:117
  7.3 312.8 %all-gather.12.cloned.1.call-start = ((), (), s32[]{:S(2)}) async-start(), calls=%async_computation.3 | async-start | bytes 11059200 | tf_op jit(solution)/shard_map/all_gather | solution.py:127
  127.0 2.8 copy-start.5
  127.0 2.8 copy-start.6
  127.0 9.1 %copy-start.7 = (s32[8]{0:T(128)S(1)}, s32[8]{0:T(128)}, u32[]{:S(2)}) copy-start(s32[8]{0:T(128)} %param.23) | copy-start | bytes 100
  127.1 299.7 %all-gather.10.cloned.1.call-start = ((), (), s32[]{:S(2)}) async-start(), calls=%async_computation.2 | async-start | bytes 5529600 | tf_op jit(solution)/shard_map/all_gather | solution.py:152
  127.8 425.5 %all-gather.8.cloned.1.call-start = ((), (), s32[]{:S(2)}) async-start(), calls=%async_computation.1 | async-start | bytes 20889600 | tf_op jit(solution)/shard_map/all_gather | solution.py:143
  330.1 1.8 copy-start.2
  331.9 0.7 copy-start.3
  331.9 1.3 copy-start.4
  553.3 25.1 %copy-start.1 = (s32[16]{0:T(128)S(1)}, s32[16]{0:T(128)}, u32[]{:S(2)}) copy-start(s32[16]{0:T(128)} %param.24) | copy-start | bytes 196
Sparse Core Ops, SparseCore 0:
  9.8 82.3 all-gather.5
  127.2 192.8 all-gather.11
  321.7 104.9 all-gather.9
  429.0 124.2 all-gather.7
where the time goes:
time: 595 us; the launch traced here: 585 us
  waiting for transfers between devices  444 us (75%)
  matrix products  61.8 us (10%)
  local copies, waits for them, and re-layouts  37.8 us (6%)
  between operations  27.8 us (5%)
  other arithmetic  11.2 us (2%)
    all_gather x1, waiting for transfers between devices, shards(): shard_piece = lax.all_gather(parent_rad, 'box', axis=1, tiled=True)  173 us
    all_gather x1, waiting for transfers between devices, shards(): shard_piece = lax.all_gather(narrowed, 'dir', axis=0, tiled=True)  98.3 us
    all_gather x1, waiting for transfers between devices, shards(): shard_piece = lax.all_gather(child_rad, 'box', axis=1, tiled=True)  91 us
    all_gather x1, waiting for transfers between devices, shards(): shard_piece = lax.all_gather(child_rad, 'dir', axis=0, tiled=True)  79.4 us
    dot_general x1, matrix products, shards(): jnp.einsum('pc,cnabt->pnabt', kernel, shard_piece, precision=highest)  25.4 us
    dot_general x1, matrix products, shards(): jnp.einsum('cp,pnabt->cnabt', kernel, shard_piece, precision=highest)  24 us
  transfers between devices with their start and end apart: 4, of which 4 were waited for; matrix products, arithmetic and copies ran while one was open for 9% of the time, Pallas kernels for 0%

commit v1 on v0

v1 whole, which is shorter than its diff:
```python
import functools
import math

import jax
import jax.numpy as jnp
import numpy as np
from jax import lax
from jax.experimental import pallas as pl
from jax.experimental.pallas import tpu as pltpu
from jax.sharding import PartitionSpec as P

T_CHILD, P_CHILD = 384, 800
T_PARENT, P_PARENT = 768, 1600
FAR_P, FAR_C = 3, 7

PARTS = 3
LANES = 128
GROUP = 7
MESH = pl.DeviceIdType.MESH
F32, BF16 = jnp.float32, jnp.bfloat16


def split_np(table):
    high = table.astype(np.float32).astype(jnp.bfloat16)
    low = (table - high.astype(np.float64)).astype(np.float32).astype(jnp.bfloat16)
    return high, low


@functools.cache
def theta_tables():
    q = np.arange(T_PARENT)
    first = np.clip((q - 1) // 2 - 2, 0, T_CHILD - 6)
    offset = q * 0.5 - 0.25 - first
    table = np.zeros((T_PARENT, T_CHILD))
    for node in range(6):
        weight = np.ones(T_PARENT)
        for other in range(6):
            if other != node:
                weight = weight * (offset - other) / (node - other)
        table[q, first + node] = weight
    part, pair, place, i = np.meshgrid(np.arange(PARTS), np.arange(32), np.arange(2), np.arange(4), indexing="ij")
    wide, narrow = [], []
    for kid in range(2):
        chip = 2 * pair + (place if kid == 0 else 1 - place)
        rows = table[(12 * chip + 4 * part + i).reshape(-1)]
        wide.append(np.stack(split_np(rows)))
        back = 0.25 * rows.reshape(PARTS, 256, T_CHILD).transpose(0, 2, 1)
        narrow.append(np.stack(split_np(back)))
    return np.stack(wide), np.stack(narrow)


@functools.cache
def phi_tables():
    p = np.arange(P_PARENT)[:, None]
    c = np.arange(P_CHILD)[None, :]
    odd = 2 * p - 4 * c - 1
    period = 4 * P_CHILD
    numerator = np.mod((P_CHILD - 1) * odd, 2 * period).astype(np.float64)
    table = np.sin(math.pi * numerator / period) / (P_CHILD * np.sin(math.pi * odd / period))
    plus = np.zeros((4 * LANES, 8 * LANES))
    minus = np.zeros((4 * LANES, 8 * LANES))
    f = np.arange(50)
    row_of = 8 * (f // GROUP) + f % GROUP
    for jj in range(4):
        for core in range(2):
            child = 100 * jj + 50 * core + f
            rows = jj * LANES + core * 64 + row_of
            for dd in range(8):
                parent = 100 * dd + np.arange(100)
                near = table[np.ix_(parent, child)].T
                far = table[np.ix_(parent, child + 400)].T
                at = np.ix_(rows, dd * LANES + np.arange(100))
                plus[at] = 0.5 * (near + far)
                minus[at] = 0.5 * (near - far)
    return np.stack([np.stack(split_np(plus)), np.stack(split_np(minus))])


@functools.cache
def phi_angles():
    lane = np.arange(16 * LANES)
    phi = 2.0 * math.pi * (100 * (lane // LANES) + lane % LANES + 0.5) / P_PARENT
    return np.stack([np.cos(phi), np.sin(phi)]).reshape(2, 1, 16 * LANES).astype(np.float32)


def split(x):
    high = x.astype(BF16)
    return high, (x - high.astype(F32)).astype(BF16)


NT = (((1,), (1,)), ((), ()))
NN = (((1,), (0,)), ((), ()))


def mul(a, b, dims):
    return lax.dot_general(a, b, dims, preferred_element_type=F32)


def kernel(
    bas, octant, far_par, far_par_off, far_child, far_child_off, far_count,
    x_in, tab_in, tabc, wide, narrow, weights, angles,
    out,
    slot_of, oct_lo, oct_hi, par_src, par_off, kid_src, kid_kid, kid_off, kid_act,
    x_swap, x_hi, x_lo, send1, recv1, send2, recv2,
    child_recv, far_out, far_recv, tab_recv, tab, etab, y, pr, r_hi, r_lo, acc, own, res_recv,
    s_swap, s_child, s_far, s_tab, s_tabf, s_main, s_back, s_loc,
):
    b = lax.axis_index("box")
    d = lax.axis_index("dir")
    core = lax.rem(d, 2)
    j = d // 2
    me = b * 8 + j
    chip_odd = lax.rem(j, 2) == 1
    buddy = (b, d + 1 - 2 * core)

    def chip(t):
        return (t // 8, lax.rem(t, 8) * 2 + core)

    barrier = pltpu.get_barrier_semaphore()
    pl.semaphore_signal(barrier, inc=1, device_id=buddy, device_id_type=MESH)

    def greet(i, carry):
        pl.semaphore_signal(barrier, inc=1, device_id=chip(lax.rem(me + i, 64)), device_id_type=MESH)
        return carry

    lax.fori_loop(1, 64, greet, 0)

    for box in range(8):
        place = jnp.int32(0)
        for s in range(8):
            place = jnp.where(bas[s] == box, s, place)
        slot_of[box] = place
    for s in range(8):
        box = bas[s]
        o0, o1 = octant[2 * box], octant[2 * box + 1]
        oct_lo[s] = jnp.where(chip_odd, o1, o0)
        oct_hi[s] = jnp.where(chip_odd, o0, o1)
        for k in range(FAR_P):
            par_src[s * FAR_P + k] = slot_of[far_par[box, k]]
            par_off[s * FAR_P + k] = far_par_off[box, k]

    def kid_entry(n, carry):
        box = bas[n // 2] * 2 + lax.rem(n, 2)
        for k in range(FAR_C):
            source = far_child[box, k]
            kid_src[n * FAR_C + k] = slot_of[source // 2]
            kid_kid[n * FAR_C + k] = lax.rem(source, 2)
            kid_off[n * FAR_C + k] = far_child_off[box, k]
            kid_act[n * FAR_C + k] = jnp.where(k < far_count[box], 1.0, 0.0).astype(F32)
        return carry

    lax.fori_loop(0, 16, kid_entry, 0)

    def own_half(c, carry):
        for k in range(2):
            high, low = split(x_in[core, c, k])
            at = pl.ds(pl.multiple_of(core * 64, 64), 64)
            x_hi[c, k, at, :] = high
            x_lo[c, k, at, :] = low
        return carry

    lax.fori_loop(0, 2, own_half, 0)

    pl.semaphore_wait(barrier, 64)

    swap = pltpu.make_async_remote_copy(
        src_ref=x_in.at[1 - core], dst_ref=x_swap, send_sem=s_swap.at[0], recv_sem=s_swap.at[1],
        device_id=buddy, device_id_type=MESH)
    swap.start()

    def child_copy(g):
        return pltpu.make_async_remote_copy(
            src_ref=x_in.at[:, :, :, pl.ds(pl.multiple_of(g * 8, 8), 8), :], dst_ref=child_recv.at[b],
            send_sem=s_child.at[0], recv_sem=s_child.at[1], device_id=(g, d), device_id_type=MESH)

    def child_start(i, carry):
        child_copy(lax.rem(b + i, 8)).start()
        return carry

    lax.fori_loop(1, 8, child_start, 0)
    child_own = pltpu.make_async_copy(
        x_in.at[:, :, :, pl.ds(pl.multiple_of(b * 8, 8), 8), :], child_recv.at[b], s_loc.at[0])
    child_own.start()

    def tab_start(i, carry):
        to = lax.rem(j + i, 8)
        pltpu.make_async_remote_copy(
            src_ref=tab_in.at[to], dst_ref=tab_recv.at[core, j], send_sem=s_tab.at[0], recv_sem=s_tab.at[1],
            device_id=(b, to * 2 + core), device_id_type=MESH).start()
        return carry

    lax.fori_loop(1, 8, tab_start, 0)
    tab_own = pltpu.make_async_copy(tab_in.at[j], tab_recv.at[core, j], s_loc.at[1])
    tab_own.start()

    swap.wait()

    def other_half(c, carry):
        for k in range(2):
            high, low = split(x_swap[c, k])
            at = pl.ds(pl.multiple_of(64 - core * 64, 64), 64)
            x_hi[c, k, at, :] = high
            x_lo[c, k, at, :] = low
        return carry

    lax.fori_loop(0, 2, other_half, 0)

    lower = lax.broadcasted_iota(jnp.int32, (8, LANES), 0) < 4

    def main_copy(part, t, send, recv, sems):
        return pltpu.make_async_remote_copy(
            src_ref=send.at[part, t], dst_ref=recv.at[part, me],
            send_sem=sems.at[0, part], recv_sem=sems.at[1, part], device_id=chip(t), device_id_type=MESH)

    def send_all(part, send, recv, sems):
        def start(i, carry):
            main_copy(part, lax.rem(me + i, 64), send, recv, sems).start()
            return carry

        lax.fori_loop(1, 64, start, 0)
        recv[part, me] = send[part, me]

    def wait_all(part, ref, sem):
        span = ref.at[part, pl.ds(0, 63)]
        pltpu.make_async_copy(span, span, sem).wait()

    def widen(part, carry):
        rows = pl.ds(pl.multiple_of(part * 256, 256), 256)
        for c in range(2):
            got = []
            for k in range(2):
                hi, lo = x_hi[c, k], x_lo[c, k]
                th, tl = wide[k, 0, rows, :], wide[k, 1, rows, :]
                got.append(mul(th, hi, NT) + mul(th, lo, NT) + mul(tl, hi, NT))
            k0 = got[0].reshape(32, 8, LANES)
            k1 = got[1].reshape(32, 8, LANES)
            m = lower[None]
            even = jnp.where(m, k0, k1)
            odd = jnp.where(m, k1, k0)
            both = jnp.stack([even, odd], axis=1).reshape(64, 8, LANES)
            send1[part, :, c * 8:c * 8 + 8, :] = both
        send_all(part, send1, recv1, s_main)
        return carry

    lax.fori_loop(0, PARTS, widen, 0)

    tab_own.wait()
    span = tab_recv.at[core, pl.ds(0, 7)]
    pltpu.make_async_copy(span, span, s_tab.at[1]).wait()
    tab_on = pltpu.make_async_remote_copy(
        src_ref=tab_recv.at[core], dst_ref=tab_recv.at[core], send_sem=s_tabf.at[0], recv_sem=s_tabf.at[1],
        device_id=buddy, device_id_type=MESH)
    tab_on.start()

    child_own.wait()
    span = child_recv.at[pl.ds(0, 7)]
    pltpu.make_async_copy(span, span, s_child.at[1]).wait()

    def far_slot(s, carry):
        for kid in range(2):
            n = s * 2 + kid
            total = [[jnp.zeros((8, T_CHILD), F32) for _ in range(2)] for _ in range(2)]
            for k in range(FAR_C):
                src, sk, off = kid_src[n * FAR_C + k], kid_kid[n * FAR_C + k], kid_off[n * FAR_C + k]
                act = kid_act[n * FAR_C + k]
                tr, ti = tabc[off, 0] * act, tabc[off, 1] * act
                for p in range(2):
                    xr, xi = child_recv[src, p, 0, sk], child_recv[src, p, 1, sk]
                    total[p][0] = total[p][0] + (tr * xr - ti * xi)
                    total[p][1] = total[p][1] + (tr * xi + ti * xr)
            for p in range(2):
                for c in range(2):
                    far_out[s, p, c, kid] = total[p][c]
        return carry

    lax.fori_loop(0, 8, far_slot, 0)

    def far_start(i, carry):
        to = lax.rem(b + i, 8)
        pltpu.make_async_remote_copy(
            src_ref=far_out.at[to], dst_ref=far_recv.at[b], send_sem=s_far.at[0], recv_sem=s_far.at[1],
            device_id=(to, d), device_id_type=MESH).start()
        return carry

    lax.fori_loop(1, 8, far_start, 0)
    far_recv[b] = far_out[b]

    tab_on.wait()

    row = lax.broadcasted_iota(jnp.int32, (8, LANES), 0)

    def one_part(part, carry):
        q = (12 * me + 4 * part + lax.rem(row, 4)).astype(F32)
        theta = (q + 0.5) * (math.pi / T_PARENT)
        st, ct = 16.0 * jnp.sin(theta), 16.0 * jnp.cos(theta)

        def prepare(blk, carry):
            at = pl.ds(pl.multiple_of(blk * LANES, LANES), LANES)
            ux, uy = st * angles[0, :, at], st * angles[1, :, at]
            for o in range(4):
                t = ct + (ux if o % 2 else -ux) + (uy if o // 2 else -uy)
                f = t - jnp.round(t)
                a = f * f
                s = f * (3.14159265358979 + a * (-5.16771278004997 + a * (2.55016403987735 + a * (
                    -0.599264529320792 + a * (0.0821458866111282 + a * (-0.00737043094571435
                    + a * 0.000466302805767613))))))
                c = 1.0 + a * (-4.93480220054468 + a * (4.05871212641677 + a * (-1.33526276885459 + a * (
                    0.235330630358893 + a * (-0.0258068913900141 + a * (0.00192957430940392
                    - a * 0.000104638104924846))))))
                cos, sin = 1.0 - 2.0 * (s * s), 2.0 * (s * c)
                etab[4 + o, 0, :, at] = cos
                etab[4 + o, 1, :, at] = sin
                etab[3 - o, 0, :, at] = cos
                etab[3 - o, 1, :, at] = -sin
            dcore, dj = lax.rem(blk, 2), blk // 2
            for off in range(8):
                v = tab_recv[dcore, dj, part, off]
                w = pltpu.roll(v, 4, 0)
                tab[off, 0, :, at] = jnp.where(lower, v, w)
                tab[off, 1, :, at] = jnp.where(lower, w, v)
            return carry

        lax.fori_loop(0, 16, prepare, 0)

        wait_all(part, recv1, s_main.at[1, part])

        got = recv1[part].reshape(8, 8, 16, LANES)
        for sign in range(2):
            pieces = []
            for jj in range(4):
                one, two = got[:, jj], got[:, jj + 4]
                pieces.append((one + two if sign == 0 else one - two).reshape(128, LANES))
            high, low = split(jnp.concatenate(pieces, axis=1))
            for n in range(4):
                cols = slice(n * 256, n * 256 + 256)
                wh, wl = weights[sign, 0, :, cols], weights[sign, 1, :, cols]
                y[sign, :, cols] = mul(high, wh, NN) + mul(low, wh, NN) + mul(high, wl, NN)

        def block(dd, carry):
            for half in range(2):
                at_y = pl.ds(pl.multiple_of(dd * LANES, LANES), LANES)
                at = pl.ds(pl.multiple_of((dd + 8 * half) * LANES, LANES), LANES)
                for s in range(8):
                    yp = y[0, s * 16:s * 16 + 16, at_y]
                    ym = y[1, s * 16:s * 16 + 16, at_y]
                    v = yp + ym if half == 0 else yp - ym
                    vr, vi = v[:8], v[8:]
                    cos = jnp.where(lower, etab[oct_lo[s], 0, :, at], etab[oct_hi[s], 0, :, at])
                    sin = jnp.where(lower, etab[oct_lo[s], 1, :, at], etab[oct_hi[s], 1, :, at])
                    re = cos * vr - sin * vi
                    im = sin * vr + cos * vi
                    pr[half, s, 0] = re + pltpu.roll(re, 4, 0)
                    pr[half, s, 1] = im + pltpu.roll(im, 4, 0)
            for s in range(8):
                back = []
                for half in range(2):
                    at = pl.ds(pl.multiple_of((dd + 8 * half) * LANES, LANES), LANES)
                    re = im = None
                    for k in range(FAR_P):
                        src, off = par_src[s * FAR_P + k], par_off[s * FAR_P + k]
                        fr, fi = pr[half, src, 0], pr[half, src, 1]
                        tr, ti = tab[off, 0, :, at], tab[off, 1, :, at]
                        gr, gi = tr * fr - ti * fi, tr * fi + ti * fr
                        re = gr if re is None else re + gr
                        im = gi if im is None else im + gi
                    cos = jnp.where(lower, etab[oct_lo[s], 0, :, at], etab[oct_hi[s], 0, :, at])
                    sin = jnp.where(lower, etab[oct_lo[s], 1, :, at], etab[oct_hi[s], 1, :, at])
                    back.append(jnp.concatenate([cos * re + sin * im, cos * im - sin * re], axis=0))
                at_y = pl.ds(pl.multiple_of(dd * LANES, LANES), LANES)
                for sign in range(2):
                    high, low = split(back[0] + back[1] if sign == 0 else back[0] - back[1])
                    r_hi[sign, s * 16:s * 16 + 16, at_y] = high
                    r_lo[sign, s * 16:s * 16 + 16, at_y] = low
            return carry

        lax.fori_loop(0, 8, block, 0)

        z = []
        for sign in range(2):
            high, low = r_hi[sign], r_lo[sign]
            wh, wl = weights[sign, 0], weights[sign, 1]
            z.append(mul(high, wh, NT) + mul(low, wh, NT) + mul(high, wl, NT))
        one, two = z[0] + z[1], z[0] - z[1]
        for jj in range(4):
            cols = slice(jj * LANES, jj * LANES + LANES)
            a = one[:, cols].reshape(8, 16, LANES)
            c = two[:, cols].reshape(8, 16, LANES)
            for s in range(8):
                send2[part, s * 8 + jj] = a[s]
                send2[part, s * 8 + jj + 4] = c[s]
        send_all(part, send2, recv2, s_back)
        return carry

    lax.fori_loop(0, PARTS, one_part, 0)

    def narrow_part(part, carry):
        wait_all(part, recv2, s_back.at[1, part])
        got = recv2[part].reshape(32, 2, 16, LANES)
        for c in range(2):
            even = got[:, 0, c * 8:c * 8 + 8]
            odd = got[:, 1, c * 8:c * 8 + 8]
            m = lower[None]
            for k in range(2):
                rows = jnp.where(m, even, odd) if k == 0 else jnp.where(m, odd, even)
                high, low = split(rows.reshape(256, LANES))
                nh, nl = narrow[k, 0, part], narrow[k, 1, part]
                term = mul(nh, high, NN) + mul(nh, low, NN) + mul(nl, high, NN)
                acc[c, k] = jnp.where(part == 0, term, acc[c, k] + term)
        return carry

    acc[...] = jnp.zeros_like(acc)
    lax.fori_loop(0, PARTS, narrow_part, 0)

    for c in range(2):
        for k in range(2):
            full = jnp.transpose(acc[c, k])
            own[0, c, k] = full[:64]
            own[1, c, k] = full[64:]
    swap2 = pltpu.make_async_remote_copy(
        src_ref=own.at[1 - core], dst_ref=res_recv, send_sem=s_swap.at[2], recv_sem=s_swap.at[3],
        device_id=buddy, device_id_type=MESH)
    swap2.start()

    span = far_recv.at[pl.ds(0, 7)]
    pltpu.make_async_copy(span, span, s_far.at[1]).wait()
    for c in range(2):
        for k in range(2):
            for g in range(8):
                rows = slice(g * 8, g * 8 + 8)
                out[core, c, k, rows, :] = own[core, c, k, rows, :] + far_recv[g, core, c, k]
    swap2.wait()
    for c in range(2):
        for k in range(2):
            for g in range(8):
                rows = slice(g * 8, g * 8 + 8)
                out[1 - core, c, k, rows, :] = res_recv[c, k, rows, :] + far_recv[g, 1 - core, c, k]

    def sent(part, carry):
        wait_all(part, send1, s_main.at[0, part])
        wait_all(part, send2, s_back.at[0, part])
        return carry

    lax.fori_loop(0, PARTS, sent, 0)
    span = child_recv.at[pl.ds(0, 7)]
    pltpu.make_async_copy(span, span, s_child.at[0]).wait()
    span = far_out.at[pl.ds(0, 7)]
    pltpu.make_async_copy(span, span, s_far.at[0]).wait()
    span = tab_in.at[pl.ds(0, 7)]
    pltpu.make_async_copy(span, span, s_tab.at[0]).wait()


def shards(child_rad, box_at_slot, octant, far_par, far_par_off, far_child, far_child_off, far_child_count,
           trans_par, trans_child):
    b = lax.axis_index("box")
    x = jnp.transpose(child_rad, (3, 2, 1, 0, 4))
    x = jnp.pad(x, ((0, 0),) * 3 + ((0, 6), (0, 0))).reshape(2, 2, 2, 8, 7, T_CHILD)
    x = jnp.pad(x, ((0, 0),) * 4 + ((0, 1), (0, 0))).reshape(2, 2, 2, 64, T_CHILD)
    t = lax.dynamic_slice_in_dim(trans_par, 96 * b, 96, 3).reshape(100, 8, 2, 8, PARTS, 4)
    t = jnp.transpose(t, (3, 4, 1, 2, 5, 0))
    t = jnp.pad(t, ((0, 0),) * 5 + ((0, LANES - 100),)).reshape(8, PARTS, 8, 8, LANES)
    tc = lax.dynamic_slice_in_dim(trans_child, jnp.minimum(GROUP * b, 42), 8, 0)
    tc = jnp.where(b == 7, tc[7:8], tc)
    tc = jnp.transpose(tc, (1, 2, 0, 3))

    wide, narrow = theta_tables()
    vmem = pl.BlockSpec(memory_space=pltpu.VMEM)
    smem = pl.BlockSpec(memory_space=pltpu.SMEM)
    out = pl.pallas_call(
        kernel,
        out_shape=jax.ShapeDtypeStruct((2, 2, 2, 64, T_CHILD), F32),
        in_specs=[smem] * 7 + [vmem] * 7,
        out_specs=vmem,
        scratch_shapes=[
            pltpu.SMEM((8,), jnp.int32),
            pltpu.SMEM((8,), jnp.int32),
            pltpu.SMEM((8,), jnp.int32),
            pltpu.SMEM((24,), jnp.int32),
            pltpu.SMEM((24,), jnp.int32),
            pltpu.SMEM((112,), jnp.int32),
            pltpu.SMEM((112,), jnp.int32),
            pltpu.SMEM((112,), jnp.int32),
            pltpu.SMEM((112,), F32),
            pltpu.VMEM((2, 2, 64, T_CHILD), F32),
            pltpu.VMEM((2, 2, 128, T_CHILD), BF16),
            pltpu.VMEM((2, 2, 128, T_CHILD), BF16),
            pltpu.VMEM((PARTS, 64, 16, LANES), F32),
            pltpu.VMEM((PARTS, 64, 16, LANES), F32),
            pltpu.VMEM((PARTS, 64, 16, LANES), F32),
            pltpu.VMEM((PARTS, 64, 16, LANES), F32),
            pltpu.VMEM((8, 2, 2, 2, 8, T_CHILD), F32),
            pltpu.VMEM((8, 2, 2, 2, 8, T_CHILD), F32),
            pltpu.VMEM((8, 2, 2, 2, 8, T_CHILD), F32),
            pltpu.VMEM((2, 8, PARTS, 8, 8, LANES), F32),
            pltpu.VMEM((8, 2, 8, 16 * LANES), F32),
            pltpu.VMEM((8, 2, 8, 16 * LANES), F32),
            pltpu.VMEM((2, 128, 8 * LANES), F32),
            pltpu.VMEM((2, 8, 2, 8, LANES), F32),
            pltpu.VMEM((2, 128, 8 * LANES), BF16),
            pltpu.VMEM((2, 128, 8 * LANES), BF16),
            pltpu.VMEM((2, 2, T_CHILD, LANES), F32),
            pltpu.VMEM((2, 2, 2, 64, T_CHILD), F32),
            pltpu.VMEM((2, 2, 64, T_CHILD), F32),
            pltpu.SemaphoreType.DMA((4,)),
            pltpu.SemaphoreType.DMA((2,)),
            pltpu.SemaphoreType.DMA((2,)),
            pltpu.SemaphoreType.DMA((2,)),
            pltpu.SemaphoreType.DMA((2,)),
            pltpu.SemaphoreType.DMA((2, PARTS)),
            pltpu.SemaphoreType.DMA((2, PARTS)),
            pltpu.SemaphoreType.DMA((2,)),
        ],
        compiler_params=pltpu.CompilerParams(
            collective_id=0, has_side_effects=True, vmem_limit_bytes=56 * 2**20),
        cost_estimate=pl.CostEstimate(flops=14_000_000_000, bytes_accessed=16_000_000, transcendentals=0),
        name="fields",
    )(box_at_slot, octant, far_par, far_par_off, far_child, far_child_off, far_child_count,
      x, t, tc, jnp.asarray(wide), jnp.asarray(narrow), jnp.asarray(phi_tables()), jnp.asarray(phi_angles()))
    out = out.reshape(2, 2, 2, 8, 8, T_CHILD)[:, :, :, :, :GROUP].reshape(2, 2, 2, 56, T_CHILD)[:, :, :, :50]
    return jnp.transpose(out, (3, 2, 1, 0, 4))


def solution(mesh):
    return jax.shard_map(
        shards,
        mesh=mesh,
        in_specs=(P("dir", "box", None, None, None), P(), P(), P(), P(), P(), P(), P(),
                  P("dir", None, None, None), P("dir", None, None, None)),
        out_specs=P("dir", "box", None, None, None),
        check_vma=False,
    )
```

time: 595 us -> 97.4 us (0.16); the launches traced: 585 us -> 97.2 us
  waiting for transfers between devices: 444 us -> 0 us
  Pallas kernels: 0 us -> 81.1 us
  matrix products: 61.8 us -> 0 us
  between operations: 27.8 us -> 0.09 us
  local copies, waits for them, and re-layouts: 37.8 us -> 15 us
  other arithmetic: 11.2 us -> 0.98 us
    all_gather x4 -> x0, waiting for transfers between devices: 442 us -> none  [the longest x1 173 us: shards(): shard_piece = lax.all_gather(parent_rad, 'box', axis=1, tiled=True)]
    pallas_call x0 -> x1, Pallas kernels: none -> 81.1 us  [shards(): pl.pallas_call(kernel, out_shape=jax.ShapeDtypeStruct((2, 2, 2, 64, T_CHI...]
    dot_general x4 -> x0, matrix products: 61.8 us -> none  [the longest x1 25.4 us: shards(): jnp.einsum('pc,cnabt->pnabt', kernel, shard_piece, precision=highest)]
    gather x13 -> x0, local copies, waits for them, and re-layouts: 23.2 us -> none  [the longest x3 11.5 us: one_entry(): picked = jnp.take(shard_piece, local_index, axis=1)]
    unnamed x19 -> x20, local copies, waits for them, and re-layouts: 0.3 us -> 7.35 us
  transfers between devices with their start and end apart: 4 -> 0, of which waited for: 4 -> 0; matrix products, arithmetic and copies ran while one was open for 9% -> 0% of each run, Pallas kernels for 0% -> 0%
where the time goes in v1:
time: 97.4 us; the launch traced here: 97.2 us
  Pallas kernels  81.1 us (83%)
  local copies, waits for them, and re-layouts  15 us (15%)
  other arithmetic  0.98 us (1%)
    pallas_call x1, Pallas kernels, shards(): pl.pallas_call(kernel, out_shape=jax.ShapeDtypeStruct((2, 2, 2, 64, T_CHI...  81.1 us
    unnamed x20, local copies, waits for them, and re-layouts  7.35 us
    dynamic_slice x1, local copies, waits for them, and re-layouts, shards(): lax.dynamic_slice_in_dim(trans_par, 96 * b, 96, 3)  2.34 us

profile of v1, /device:TPU:1, one launch (start us, length us, event | category | flops | bytes accessed | tf_op | source)
XLA Modules:
  0.0 97.2 jit_solution(13914936250282311843)
XLA Ops:
  0.0 0.0 copy-start
  0.0 1.7 %copy-done = f32[50,16,2,384]{3,2,1,0:T(2,128)S(1)} copy-done((f32[50,16,2,384]{3,2,1,0:T(2,128)S(1)}, f32[50,16,2,384]{3,2,1,0:T(2,128)}, u32[]{:S(2)}) %copy-start) | copy-done | bytes 2457624
  1.7 0.1 constant_dynamic-slice_fusion
  1.8 0.1 copy.37
  1.9 1.0 %select_bitcast_fusion.tabc = f32[16,2,8,384]{3,2,1,0:T(8,128)} fusion(f32[16,2,384]{2,1,0:T(2,128)S(1)} %bitcast.24, pred[]{:T(512)S(6)} %eq.3, f32[8,16,2,384]{3,2,1,0:T(2,128)S(1)} %constant_dynamic-slice_fusion), kind=kLoop, calls=%fused_computation.2 | loop fusion | flops 98304 | bytes 835585 | tf_op jit(solution)/shard_map/transpose | solution.py:462
  2.9 2.3 %constant_dynamic-slice_fusion.1 = f32[100,8,2,96]{3,2,1,0:T(2,128)S(1)} fusion(f32[100,8,2,768]{3,2,1,0:T(2,128)} %param.22, s32[]{:T(128)S(6)} %select_n.14), kind=kLoop, calls=%fused_computation.5 | loop fusion | bytes 1228804 | tf_op jit(solution)/shard_map/dynamic_slice | solution.py:457
  5.2 1.4 %copy.33 = f32[100,8,2,96]{0,1,3,2:T(8,128)} copy(f32[100,8,2,96]{3,2,1,0:T(2,128)S(1)} %constant_dynamic-slice_fusion.1) | data formatting | bytes 1228800
  6.7 0.0 copy-start.1
  6.7 1.4 %copy.34 = f32[8,3,8,2,4,100]{5,4,3,2,1,0:T(4,128)S(1)} copy(f32[8,3,8,2,4,100]{5,2,4,1,0,3:T(8,128)} %bitcast.18) | data formatting | bytes 1228800
  8.1 1.1 %pad.14.clone = f32[8,3,8,2,4,128]{5,4,3,2,1,0:T(4,128)} pad(f32[8,3,8,2,4,100]{5,4,3,2,1,0:T(4,128)S(1)} %copy.34, f32[]{:T(128)} %constant.7.clone.1), padding=0_0x0_0x0_0x0_0x0_0x0_28 | pad | bytes 1400836 | tf_op jit(solution)/shard_map/jit(_pad)/pad | solution.py:459
  9.2 0.0 copy-start.2
  9.2 0.0 copy-start.3
  9.2 0.0 copy-start.4
  9.2 0.0 copy-start.5
  9.2 0.0 copy-done.1
  9.3 0.2 pad.12
  9.5 0.2 copy.22
  9.7 1.0 pad_bitcast_fusion.x_in
  10.6 0.0 copy-done.2
  10.6 0.7 copy.28.far_child
  11.3 0.0 copy-done.3
  11.3 0.7 copy.29.far_child_off
  12.0 0.0 copy-done.4
  12.0 0.7 copy.26.far_par
  12.6 0.0 copy-done.5
  12.6 0.7 copy.27.far_par_off
  13.3 81.1 %fields.1 = f32[2,2,2,64,384]{4,3,2,1,0:T(8,128)} custom-call(s32[8]{0:T(128)} %bas.1, s32[16]{0:T(128)} %octant.1, s32[8,3]{1,0:T(8,128)} %copy.26.far_par, s32[8,3]{1,0:T(8,128)} %copy.27.far_par_off, s32[16,7]{1,0:T(8,128)} %copy.28.far_child, s32[16,7]{1,0:T(8,128)} %copy.29.far_child_off, s32[16]{0:T(128)} %far_count.1, ...), custom_call_target="tpu_custom_call" | custom-call | flops 14000000000 | bytes 16000000 | tf_op jit(solution)/shard_map/fields/pallas_call | solution.py:467
  94.5 1.7 %copy.30 = f32[2,2,2,8,7,384]{5,0,1,2,4,3:T(2,128)S(1)} copy(f32[2,2,2,8,7,384]{5,4,3,2,1,0:T(8,128)} %bitcast.22) | data formatting | bytes 1376256 | tf_op jit(solution)/shard_map/slice | solution.py:517
  96.1 1.0 %slice_bitcast_fusion = f32[50,2,2,2,384]{4,3,2,1,0:T(2,128)} fusion(f32[2,2,2,56,384]{4,0,1,2,3:T(2,128)S(1)} %bitcast.20), kind=kLoop, calls=%fused_computation.1 | loop fusion | bytes 1228800 | tf_op jit(solution)/shard_map/transpose | solution.py:518
  (2 shorter events, 0.0 us)
Async XLA Ops:
  0.0 1.7 %copy-start = (f32[50,16,2,384]{3,2,1,0:T(2,128)S(1)}, f32[50,16,2,384]{3,2,1,0:T(2,128)}, u32[]{:S(2)}) copy-start(f32[50,16,2,384]{3,2,1,0:T(2,128)} %param.23) | copy-start | bytes 7372804
  6.7 2.6 %copy-start.1 = (f32[50,2,2,2,384]{4,3,2,1,0:T(2,128)S(1)}, f32[50,2,2,2,384]{4,3,2,1,0:T(2,128)}, u32[]{:S(2)}) copy-start(f32[50,2,2,2,384]{4,3,2,1,0:T(2,128)} %param.14) | copy-start | bytes 1843204
  9.2 1.4 %copy-start.2 = (s32[16,7]{0,1:T(8,128)S(1)}, s32[16,7]{0,1:T(8,128)}, u32[]{:S(2)}) copy-start(s32[16,7]{0,1:T(8,128)} %param.19) | copy-start | bytes 1348
  9.2 2.1 %copy-start.3 = (s32[16,7]{0,1:T(8,128)S(1)}, s32[16,7]{0,1:T(8,128)}, u32[]{:S(2)}) copy-start(s32[16,7]{0,1:T(8,128)} %param.20) | copy-start | bytes 1348
  9.2 2.7 %copy-start.4 = (s32[8,3]{0,1:T(4,128)S(1)}, s32[8,3]{0,1:T(4,128)}, u32[]{:S(2)}) copy-start(s32[8,3]{0,1:T(4,128)} %param.17) | copy-start | bytes 292
  9.2 3.4 %copy-start.5 = (s32[8,3]{0,1:T(4,128)S(1)}, s32[8,3]{0,1:T(4,128)}, u32[]{:S(2)}) copy-start(s32[8,3]{0,1:T(4,128)} %param.18) | copy-start | bytes 292

commit v2 on v1

--- a/solution.py
+++ b/solution.py
@@ -60,11 +60,10 @@
     plus = np.zeros((4 * LANES, 8 * LANES))
     minus = np.zeros((4 * LANES, 8 * LANES))
     f = np.arange(50)
-    row_of = 8 * (f // GROUP) + f % GROUP
     for jj in range(4):
         for core in range(2):
             child = 100 * jj + 50 * core + f
-            rows = jj * LANES + core * 64 + row_of
+            rows = jj * LANES + core * 50 + f
             for dd in range(8):
                 parent = 100 * dd + np.arange(100)
                 near = table[np.ix_(parent, child)].T
@@ -97,12 +96,14 @@
 
 def kernel(
     bas, octant, far_par, far_par_off, far_child, far_child_off, far_count,
-    x_in, tab_in, tabc, wide, narrow, weights, angles,
+    x_hbm, tab_hbm, tabc_hbm, wide_hbm, narrow_hbm, weights_hbm, angles,
     out,
     slot_of, oct_lo, oct_hi, par_src, par_off, kid_src, kid_kid, kid_off, kid_act,
-    x_swap, x_hi, x_lo, send1, recv1, send2, recv2,
-    child_recv, far_out, far_recv, tab_recv, tab, etab, y, pr, r_hi, r_lo, acc, own, res_recv,
-    s_swap, s_child, s_far, s_tab, s_tabf, s_main, s_back, s_loc,
+    x_raw, tab_raw, tabc_raw, wide, narrow, weights,
+    xf, x_swap, x_hi, x_lo, send1, recv1, send2, recv2,
+    child_recv, child, tabc, far_out, far_recv, far, tv, tab_send, tab_recv, tab, etab, y, pr, r_hi, r_lo, acc, own,
+    res_recv,
+    s_in, s_swap, s_child, s_far, s_tab, s_tabf, s_main, s_back, s_loc,
 ):
     b = lax.axis_index("box")
     d = lax.axis_index("dir")
@@ -122,7 +123,20 @@
         pl.semaphore_signal(barrier, inc=1, device_id=chip(lax.rem(me + i, 64)), device_id_type=MESH)
         return carry
 
+    group = jnp.minimum(GROUP * b, 50 - GROUP)
+    window = pl.multiple_of((3 * (b // 2)) // 2 * LANES, LANES)
+    loads = [
+        pltpu.make_async_copy(x_hbm, x_raw, s_in.at[0]),
+        pltpu.make_async_copy(wide_hbm, wide, s_in.at[1]),
+        pltpu.make_async_copy(tab_hbm.at[:, :, :, pl.ds(window, 256)], tab_raw, s_in.at[2]),
+        pltpu.make_async_copy(tabc_hbm.at[pl.ds(group, GROUP)], tabc_raw, s_in.at[3]),
+        pltpu.make_async_copy(weights_hbm, weights, s_in.at[4]),
+        pltpu.make_async_copy(narrow_hbm, narrow, s_in.at[5]),
+    ]
+    loads[0].start()
     lax.fori_loop(1, 64, greet, 0)
+    for load in loads[1:]:
+        load.start()
 
     for box in range(8):
         place = jnp.int32(0)
@@ -135,93 +149,140 @@
         oct_lo[s] = jnp.where(chip_odd, o1, o0)
         oct_hi[s] = jnp.where(chip_odd, o0, o1)
         for k in range(FAR_P):
-            par_src[s * FAR_P + k] = slot_of[far_par[box, k]]
-            par_off[s * FAR_P + k] = far_par_off[box, k]
+            par_src[s * FAR_P + k] = slot_of[far_par[k, box]]
+            par_off[s * FAR_P + k] = far_par_off[k, box]
 
     def kid_entry(n, carry):
         box = bas[n // 2] * 2 + lax.rem(n, 2)
         for k in range(FAR_C):
-            source = far_child[box, k]
+            source = far_child[k, box]
             kid_src[n * FAR_C + k] = slot_of[source // 2]
             kid_kid[n * FAR_C + k] = lax.rem(source, 2)
-            kid_off[n * FAR_C + k] = far_child_off[box, k]
+            kid_off[n * FAR_C + k] = far_child_off[k, box]
             kid_act[n * FAR_C + k] = jnp.where(k < far_count[box], 1.0, 0.0).astype(F32)
         return carry
 
-    lax.fori_loop(0, 16, kid_entry, 0)
-
-    def own_half(c, carry):
-        for k in range(2):
-            high, low = split(x_in[core, c, k])
-            at = pl.ds(pl.multiple_of(core * 64, 64), 64)
-            x_hi[c, k, at, :] = high
-            x_lo[c, k, at, :] = low
-        return carry
-
-    lax.fori_loop(0, 2, own_half, 0)
+    loads[0].wait()
+    for p in range(2):
+        for c in range(2):
+            for k in range(2):
+                xf[p, c, k, 0:50, :] = x_raw[:, k, c, p, :]
 
     pl.semaphore_wait(barrier, 64)
 
     swap = pltpu.make_async_remote_copy(
-        src_ref=x_in.at[1 - core], dst_ref=x_swap, send_sem=s_swap.at[0], recv_sem=s_swap.at[1],
+        src_ref=xf.at[1 - core], dst_ref=x_swap, send_sem=s_swap.at[0], recv_sem=s_swap.at[1],
         device_id=buddy, device_id_type=MESH)
     swap.start()
 
-    def child_copy(g):
-        return pltpu.make_async_remote_copy(
-            src_ref=x_in.at[:, :, :, pl.ds(pl.multiple_of(g * 8, 8), 8), :], dst_ref=child_recv.at[b],
-            send_sem=s_child.at[0], recv_sem=s_child.at[1], device_id=(g, d), device_id_type=MESH)
-
     def child_start(i, carry):
-        child_copy(lax.rem(b + i, 8)).start()
+        g = lax.rem(b + i, 8)
+        pltpu.make_async_remote_copy(
+            src_ref=x_raw.at[pl.ds(jnp.minimum(GROUP * g, 50 - GROUP), GROUP)], dst_ref=child_recv.at[b],
+            send_sem=s_child.at[0], recv_sem=s_child.at[1], device_id=(g, d), device_id_type=MESH).start()
         return carry
 
     lax.fori_loop(1, 8, child_start, 0)
-    child_own = pltpu.make_async_copy(
-        x_in.at[:, :, :, pl.ds(pl.multiple_of(b * 8, 8), 8), :], child_recv.at[b], s_loc.at[0])
+    child_own = pltpu.make_async_copy(x_raw.at[pl.ds(group, GROUP)], child_recv.at[b], s_loc.at[0])
     child_own.start()
 
-    def tab_start(i, carry):
-        to = lax.rem(j + i, 8)
-        pltpu.make_async_remote_copy(
-            src_ref=tab_in.at[to], dst_ref=tab_recv.at[core, j], send_sem=s_tab.at[0], recv_sem=s_tab.at[1],
-            device_id=(b, to * 2 + core), device_id_type=MESH).start()
-        return carry
-
-    lax.fori_loop(1, 8, tab_start, 0)
-    tab_own = pltpu.make_async_copy(tab_in.at[j], tab_recv.at[core, j], s_loc.at[1])
-    tab_own.start()
+    lax.fori_loop(0, 16, kid_entry, 0)
+
+    lower = lax.broadcasted_iota(jnp.int32, (8, LANES), 0) < 4
+    lane = lax.broadcasted_iota(jnp.int32, (8, LANES), 1)
+
+    y_hi, x_at = j // 4, lax.rem(j, 4)
+    other_box = b + 1 - 2 * lax.rem(b, 2)
+    first_chip = [b * 8 + y_hi * 4, other_box * 8 + (1 - y_hi) * 4]
+    rows = lax.broadcasted_iota(jnp.int32, (96, 256), 0)
+    columns = lax.broadcasted_iota(jnp.int32, (96, 256), 1)
+    sets = (rows >= 48).astype(jnp.int32)
+    parts = (rows >> 4) - 3 * sets
+    place = (rows >> 2) & 3
+    theta_at = 12 * (jnp.where(rows >= 48, first_chip[1], first_chip[0]) + place) + 4 * parts + (rows & 3) - window
+    swapped = theta_at + jnp.where((place & 1) == 0, 12, -12)
+    picks = [(columns == q).astype(F32).astype(BF16) for q in (theta_at, swapped)]
+    loads[2].wait()
+    tv[...] = jnp.zeros_like(tv)
+
+    def tab_prepare(off, carry):
+        got = []
+        for c in range(2):
+            tv[c, 0:100, :] = tab_raw[:, off, c, :]
+            high, low = split(tv[c])
+            got.append((mul(picks[c], high, NT) + mul(picks[c], low, NT)).reshape(2, 3, 2, 2, 4, LANES))
+        flat = [g.reshape(12, 8, LANES) for g in got]
+        even = jnp.where(lower[None], flat[0], flat[1]).reshape(2, 3, 2, 8, LANES)
+        odd = jnp.where(lower[None], flat[1], flat[0]).reshape(2, 3, 2, 8, LANES)
+        for s in range(2):
+            for u in range(2):
+                tab_send[s, 2 * u, :, off] = even[s, :, u]
+                tab_send[s, 2 * u + 1, :, off] = odd[s, :, u]
+        return carry
+
+    lax.fori_loop(0, 8, tab_prepare, 0)
+
+    def tab_start(x, carry):
+        def go(s):
+            box = b if s == 0 else other_box
+            half = y_hi if s == 0 else 1 - y_hi
+            pltpu.make_async_remote_copy(
+                src_ref=tab_send.at[s, x], dst_ref=tab_recv.at[core, j], send_sem=s_tab.at[0], recv_sem=s_tab.at[1],
+                device_id=(box, (half * 4 + x) * 2 + core), device_id_type=MESH).start()
+
+        go(1)
+
+        @pl.when(x != x_at)
+        def _():
+            go(0)
+
+        return carry
+
+    lax.fori_loop(0, 4, tab_start, 0)
+    tab_recv[core, j] = tab_send[0, x_at]
 
     swap.wait()
 
-    def other_half(c, carry):
+    def gather_rows(c, carry):
         for k in range(2):
-            high, low = split(x_swap[c, k])
-            at = pl.ds(pl.multiple_of(64 - core * 64, 64), 64)
-            x_hi[c, k, at, :] = high
-            x_lo[c, k, at, :] = low
-        return carry
-
-    lax.fori_loop(0, 2, other_half, 0)
-
-    lower = lax.broadcasted_iota(jnp.int32, (8, LANES), 0) < 4
-
-    def main_copy(part, t, send, recv, sems):
-        return pltpu.make_async_remote_copy(
-            src_ref=send.at[part, t], dst_ref=recv.at[part, me],
-            send_sem=sems.at[0, part], recv_sem=sems.at[1, part], device_id=chip(t), device_id_type=MESH)
-
-    def send_all(part, send, recv, sems):
+            mine, other = xf[core, c, k, 0:50, :], x_swap[c, k, 0:50, :]
+            zero = core == 0
+            full = jnp.concatenate(
+                [jnp.where(zero, mine, other), jnp.where(zero, other, mine), jnp.zeros((28, T_CHILD), F32)], axis=0)
+            high, low = split(full)
+            x_hi[c, k] = high
+            x_lo[c, k] = low
+        return carry
+
+    lax.fori_loop(0, 2, gather_rows, 0)
+    loads[1].wait()
+
+    def send_all(part, count, send, recv, sems):
         def start(i, carry):
-            main_copy(part, lax.rem(me + i, 64), send, recv, sems).start()
+            t = lax.rem(me + i, 64)
+            pltpu.make_async_remote_copy(
+                src_ref=send.at[part, t, pl.ds(0, count)], dst_ref=recv.at[part, me, pl.ds(0, count)],
+                send_sem=sems.at[0, part], recv_sem=sems.at[1, part], device_id=chip(t), device_id_type=MESH).start()
             return carry
 
         lax.fori_loop(1, 64, start, 0)
         recv[part, me] = send[part, me]
 
-    def wait_all(part, ref, sem):
-        span = ref.at[part, pl.ds(0, 63)]
+    def wait_all(part, count, ref, sem):
+        span = ref.at[part, pl.ds(0, 63), pl.ds(0, count)]
         pltpu.make_async_copy(span, span, sem).wait()
+
+    spare = (lane >= 100) & (lane < 125)
+
+    def stow(m, tile, extra):
+        shape = tile.shape
+        moved = pltpu.roll(extra.reshape(-1, LANES), 100 - 25 * m, 1).reshape(shape)
+        return jnp.where(spare[None], moved, tile)
+
+    def unstow(m, tile, extra):
+        shape = tile.shape
+        moved = pltpu.roll(tile.reshape(-1, LANES), 28 + 25 * m, 1).reshape(shape)
+        return jnp.where(((lane >= 25 * m) & (lane < 25 * m + 25))[None], moved, extra)
 
     def widen(part, carry):
         rows = pl.ds(pl.multiple_of(part * 256, 256), 256)
@@ -238,52 +299,83 @@
             odd = jnp.where(m, k1, k0)
             both = jnp.stack([even, odd], axis=1).reshape(64, 8, LANES)
             send1[part, :, c * 8:c * 8 + 8, :] = both
-        send_all(part, send1, recv1, s_main)
         return carry
 
     lax.fori_loop(0, PARTS, widen, 0)
 
-    tab_own.wait()
+    def stow_forward(i, carry):
+        at = pl.ds(i * 8, 8)
+        extra = send1[2, at, 8:16, :]
+        for m in range(4):
+            half = slice(8 * (m % 2), 8 * (m % 2) + 8)
+            send1[m // 2, at, half, :] = stow(m, send1[m // 2, at, half, :], extra)
+        return carry
+
+    lax.fori_loop(0, 8, stow_forward, 0)
+
+    def send_forward(part, carry):
+        send_all(part, 16, send1, recv1, s_main)
+        return carry
+
+    lax.fori_loop(0, 2, send_forward, 0)
+    send_all(2, 8, send1, recv1, s_main)
+
+    loads[3].wait()
+    for off in range(16):
+        for c in range(2):
+            tabc[off, c, 0:GROUP, :] = tabc_raw[:, off, c, :]
+    child_own.wait()
+    span = child_recv.at[pl.ds(0, 7)]
+    pltpu.make_async_copy(span, span, s_child.at[1]).wait()
+
+    def child_rows(src, carry):
+        for p in range(2):
+            for c in range(2):
+                for k in range(2):
+                    child[src, p, c, k, 0:GROUP, :] = child_recv[src, :, k, c, p, :]
+        return carry
+
+    lax.fori_loop(0, 8, child_rows, 0)
+
+    def far_slot(s, carry):
+        for kid in range(2):
+            n = s * 2 + kid
+            total = [[jnp.zeros((GROUP, T_CHILD), F32) for _ in range(2)] for _ in range(2)]
+            for k in range(FAR_C):
+                src, sk, off = kid_src[n * FAR_C + k], kid_kid[n * FAR_C + k], kid_off[n * FAR_C + k]
+                act = kid_act[n * FAR_C + k]
+                tr, ti = tabc[off, 0, 0:GROUP, :] * act, tabc[off, 1, 0:GROUP, :] * act
+                for p in range(2):
+                    xr, xi = child[src, p, 0, sk, 0:GROUP, :], child[src, p, 1, sk, 0:GROUP, :]
+                    total[p][0] = total[p][0] + (tr * xr - ti * xi)
+                    total[p][1] = total[p][1] + (tr * xi + ti * xr)
+            for p in range(2):
+                for c in range(2):
+                    far_out[s, 0:GROUP, kid, c, p, :] = total[p][c]
+        return carry
+
+    lax.fori_loop(0, 8, far_slot, 0)
+
+    far_row = jnp.where(b == 7, GROUP - 1, 0)
+
+    def far_start(i, carry):
+        to = lax.rem(b + i, 8)
+        pltpu.make_async_remote_copy(
+            src_ref=far_out.at[to, pl.ds(far_row, GROUP)], dst_ref=far_recv.at[b],
+            send_sem=s_far.at[0], recv_sem=s_far.at[1], device_id=(to, d), device_id_type=MESH).start()
+        return carry
+
+    lax.fori_loop(1, 8, far_start, 0)
+    far_own = pltpu.make_async_copy(far_out.at[b, pl.ds(far_row, GROUP)], far_recv.at[b], s_loc.at[1])
+    far_own.start()
+
     span = tab_recv.at[core, pl.ds(0, 7)]
     pltpu.make_async_copy(span, span, s_tab.at[1]).wait()
     tab_on = pltpu.make_async_remote_copy(
         src_ref=tab_recv.at[core], dst_ref=tab_recv.at[core], send_sem=s_tabf.at[0], recv_sem=s_tabf.at[1],
         device_id=buddy, device_id_type=MESH)
     tab_on.start()
-
-    child_own.wait()
-    span = child_recv.at[pl.ds(0, 7)]
-    pltpu.make_async_copy(span, span, s_child.at[1]).wait()
-
-    def far_slot(s, carry):
-        for kid in range(2):
-            n = s * 2 + kid
-            total = [[jnp.zeros((8, T_CHILD), F32) for _ in range(2)] for _ in range(2)]
-            for k in range(FAR_C):
-                src, sk, off = kid_src[n * FAR_C + k], kid_kid[n * FAR_C + k], kid_off[n * FAR_C + k]
-                act = kid_act[n * FAR_C + k]
-                tr, ti = tabc[off, 0] * act, tabc[off, 1] * act
-                for p in range(2):
-                    xr, xi = child_recv[src, p, 0, sk], child_recv[src, p, 1, sk]
-                    total[p][0] = total[p][0] + (tr * xr - ti * xi)
-                    total[p][1] = total[p][1] + (tr * xi + ti * xr)
-            for p in range(2):
-                for c in range(2):
-                    far_out[s, p, c, kid] = total[p][c]
-        return carry
-
-    lax.fori_loop(0, 8, far_slot, 0)
-
-    def far_start(i, carry):
-        to = lax.rem(b + i, 8)
-        pltpu.make_async_remote_copy(
-            src_ref=far_out.at[to], dst_ref=far_recv.at[b], send_sem=s_far.at[0], recv_sem=s_far.at[1],
-            device_id=(to, d), device_id_type=MESH).start()
-        return carry
-
-    lax.fori_loop(1, 8, far_start, 0)
-    far_recv[b] = far_out[b]
-
+    loads[4].wait()
     tab_on.wait()
 
     row = lax.broadcasted_iota(jnp.int32, (8, LANES), 0)
@@ -315,13 +407,31 @@
             for off in range(8):
                 v = tab_recv[dcore, dj, part, off]
                 w = pltpu.roll(v, 4, 0)
-                tab[off, 0, :, at] = jnp.where(lower, v, w)
-                tab[off, 1, :, at] = jnp.where(lower, w, v)
+                one = jnp.where(lower, v, w)
+                two = jnp.where(lower, w, v)
+                tab[off, 0, :, at] = jnp.where(chip_odd, two, one)
+                tab[off, 1, :, at] = jnp.where(chip_odd, one, two)
             return carry
 
         lax.fori_loop(0, 16, prepare, 0)
 
-        wait_all(part, recv1, s_main.at[1, part])
+        @pl.when(part < 2)
+        def _():
+            wait_all(part, 16, recv1, s_main.at[1, part])
+
+        @pl.when(part == 2)
+        def _():
+            wait_all(2, 8, recv1, s_main.at[1, 2])
+
+            def take(i, carry):
+                at = pl.ds(i * 8, 8)
+                extra = jnp.zeros((8, 8, LANES), F32)
+                for m in range(4):
+                    extra = unstow(m, recv1[m // 2, at, 8 * (m % 2):8 * (m % 2) + 8, :], extra)
+                recv1[2, at, 8:16, :] = extra
+                return carry
+
+            lax.fori_loop(0, 8, take, 0)
 
         got = recv1[part].reshape(8, 8, 16, LANES)
         for sign in range(2):
@@ -387,87 +497,119 @@
             for s in range(8):
                 send2[part, s * 8 + jj] = a[s]
                 send2[part, s * 8 + jj + 4] = c[s]
-        send_all(part, send2, recv2, s_back)
+
+        for at_part in range(PARTS):
+            @pl.when(part == at_part)
+            def _():
+                if at_part > 0:
+                    def stow_back(i, carry):
+                        at = pl.ds(i * 8, 8)
+                        extra = send2[0, at, 8:16, :]
+                        for h in range(2):
+                            half = slice(8 * h, 8 * h + 8)
+                            send2[at_part, at, half, :] = stow(
+                                2 * at_part - 2 + h, send2[at_part, at, half, :], extra)
+                        return carry
+
+                    lax.fori_loop(0, 8, stow_back, 0)
+                send_all(at_part, 16 if at_part > 0 else 8, send2, recv2, s_back)
+
         return carry
 
     lax.fori_loop(0, PARTS, one_part, 0)
 
+    far_own.wait()
+    span = far_recv.at[pl.ds(0, 7)]
+    pltpu.make_async_copy(span, span, s_far.at[1]).wait()
+    for p in range(2):
+        for c in range(2):
+            for k in range(2):
+                for g in range(8):
+                    count = GROUP if g < 7 else 1
+                    far[p, c, k, g * GROUP:g * GROUP + count, :] = far_recv[g, 0:count, k, c, p, :]
+
+    loads[5].wait()
+    acc[...] = jnp.zeros_like(acc)
+
+    def narrow_tile(part, c):
+        got = recv2[part, :, c * 8:c * 8 + 8, :].reshape(32, 2, 8, LANES)
+        even, odd = got[:, 0], got[:, 1]
+        m = lower[None]
+        for k in range(2):
+            rows = jnp.where(m, even, odd) if k == 0 else jnp.where(m, odd, even)
+            high, low = split(rows.reshape(256, LANES))
+            nh, nl = narrow[k, 0, part], narrow[k, 1, part]
+            acc[c, k] = acc[c, k] + (mul(nh, high, NN) + mul(nh, low, NN) + mul(nl, high, NN))
+
+    wait_all(0, 8, recv2, s_back.at[1, 0])
+    narrow_tile(0, 0)
+
     def narrow_part(part, carry):
-        wait_all(part, recv2, s_back.at[1, part])
-        got = recv2[part].reshape(32, 2, 16, LANES)
+        wait_all(part, 16, recv2, s_back.at[1, part])
         for c in range(2):
-            even = got[:, 0, c * 8:c * 8 + 8]
-            odd = got[:, 1, c * 8:c * 8 + 8]
-            m = lower[None]
-            for k in range(2):
-                rows = jnp.where(m, even, odd) if k == 0 else jnp.where(m, odd, even)
-                high, low = split(rows.reshape(256, LANES))
-                nh, nl = narrow[k, 0, part], narrow[k, 1, part]
-                term = mul(nh, high, NN) + mul(nh, low, NN) + mul(nl, high, NN)
-                acc[c, k] = jnp.where(part == 0, term, acc[c, k] + term)
-        return carry
-
-    acc[...] = jnp.zeros_like(acc)
-    lax.fori_loop(0, PARTS, narrow_part, 0)
+            narrow_tile(part, c)
+        return carry
+
+    lax.fori_loop(1, PARTS, narrow_part, 0)
+
+    def take_back(i, carry):
+        at = pl.ds(i * 8, 8)
+        extra = jnp.zeros((8, 8, LANES), F32)
+        for m in range(4):
+            extra = unstow(m, recv2[1 + m // 2, at, 8 * (m % 2):8 * (m % 2) + 8, :], extra)
+        recv2[0, at, 8:16, :] = extra
+        return carry
+
+    lax.fori_loop(0, 8, take_back, 0)
+    narrow_tile(0, 1)
 
     for c in range(2):
         for k in range(2):
             full = jnp.transpose(acc[c, k])
-            own[0, c, k] = full[:64]
-            own[1, c, k] = full[64:]
+            own[0, c, k, 0:50, :] = full[0:50]
+            own[1, c, k, 0:50, :] = full[50:100]
     swap2 = pltpu.make_async_remote_copy(
         src_ref=own.at[1 - core], dst_ref=res_recv, send_sem=s_swap.at[2], recv_sem=s_swap.at[3],
         device_id=buddy, device_id_type=MESH)
     swap2.start()
-
-    span = far_recv.at[pl.ds(0, 7)]
-    pltpu.make_async_copy(span, span, s_far.at[1]).wait()
-    for c in range(2):
-        for k in range(2):
-            for g in range(8):
-                rows = slice(g * 8, g * 8 + 8)
-                out[core, c, k, rows, :] = own[core, c, k, rows, :] + far_recv[g, core, c, k]
+    for p in range(2):
+        @pl.when(core == p)
+        def _():
+            for c in range(2):
+                for k in range(2):
+                    out[:, k, c, p, :] = own[p, c, k, 0:50, :] + far[p, c, k, 0:50, :]
+
     swap2.wait()
-    for c in range(2):
-        for k in range(2):
-            for g in range(8):
-                rows = slice(g * 8, g * 8 + 8)
-                out[1 - core, c, k, rows, :] = res_recv[c, k, rows, :] + far_recv[g, 1 - core, c, k]
-
-    def sent(part, carry):
-        wait_all(part, send1, s_main.at[0, part])
-        wait_all(part, send2, s_back.at[0, part])
-        return carry
-
-    lax.fori_loop(0, PARTS, sent, 0)
+    for p in range(2):
+        @pl.when(core != p)
+        def _():
+            for c in range(2):
+                for k in range(2):
+                    out[:, k, c, p, :] = res_recv[c, k, 0:50, :] + far[p, c, k, 0:50, :]
+
+    for part in range(PARTS):
+        wait_all(part, 8 if part == 2 else 16, send1, s_main.at[0, part])
+        wait_all(part, 8 if part == 0 else 16, send2, s_back.at[0, part])
     span = child_recv.at[pl.ds(0, 7)]
     pltpu.make_async_copy(span, span, s_child.at[0]).wait()
-    span = far_out.at[pl.ds(0, 7)]
+    span = far_recv.at[pl.ds(0, 7)]
     pltpu.make_async_copy(span, span, s_far.at[0]).wait()
-    span = tab_in.at[pl.ds(0, 7)]
+    span = tab_recv.at[core, pl.ds(0, 7)]
     pltpu.make_async_copy(span, span, s_tab.at[0]).wait()
 
 
 def shards(child_rad, box_at_slot, octant, far_par, far_par_off, far_child, far_child_off, far_child_count,
            trans_par, trans_child):
-    b = lax.axis_index("box")
-    x = jnp.transpose(child_rad, (3, 2, 1, 0, 4))
-    x = jnp.pad(x, ((0, 0),) * 3 + ((0, 6), (0, 0))).reshape(2, 2, 2, 8, 7, T_CHILD)
-    x = jnp.pad(x, ((0, 0),) * 4 + ((0, 1), (0, 0))).reshape(2, 2, 2, 64, T_CHILD)
-    t = lax.dynamic_slice_in_dim(trans_par, 96 * b, 96, 3).reshape(100, 8, 2, 8, PARTS, 4)
-    t = jnp.transpose(t, (3, 4, 1, 2, 5, 0))
-    t = jnp.pad(t, ((0, 0),) * 5 + ((0, LANES - 100),)).reshape(8, PARTS, 8, 8, LANES)
-    tc = lax.dynamic_slice_in_dim(trans_child, jnp.minimum(GROUP * b, 42), 8, 0)
-    tc = jnp.where(b == 7, tc[7:8], tc)
-    tc = jnp.transpose(tc, (1, 2, 0, 3))
-
     wide, narrow = theta_tables()
     vmem = pl.BlockSpec(memory_space=pltpu.VMEM)
     smem = pl.BlockSpec(memory_space=pltpu.SMEM)
-    out = pl.pallas_call(
+    anywhere = pl.BlockSpec(memory_space=pl.ANY)
+    chunks = pltpu.VMEM((PARTS, 64, 16, LANES), F32)
+    groups = pltpu.VMEM((8, GROUP, 2, 2, 2, T_CHILD), F32)
+    return pl.pallas_call(
         kernel,
-        out_shape=jax.ShapeDtypeStruct((2, 2, 2, 64, T_CHILD), F32),
-        in_specs=[smem] * 7 + [vmem] * 7,
+        out_shape=jax.ShapeDtypeStruct((50, 2, 2, 2, T_CHILD), F32),
+        in_specs=[smem] * 7 + [anywhere] * 6 + [vmem],
         out_specs=vmem,
         scratch_shapes=[
             pltpu.SMEM((8,), jnp.int32),
@@ -479,16 +621,25 @@
             pltpu.SMEM((112,), jnp.int32),
             pltpu.SMEM((112,), jnp.int32),
             pltpu.SMEM((112,), F32),
-            pltpu.VMEM((2, 2, 64, T_CHILD), F32),
+            pltpu.VMEM((50, 2, 2, 2, T_CHILD), F32),
+            pltpu.VMEM((100, 8, 2, 256), F32),
+            pltpu.VMEM((GROUP, 16, 2, T_CHILD), F32),
+            pltpu.VMEM(wide.shape, BF16),
+            pltpu.VMEM(narrow.shape, BF16),
+            pltpu.VMEM((2, 2, 4 * LANES, 8 * LANES), BF16),
+            pltpu.VMEM((2, 2, 2, 56, T_CHILD), F32),
+            pltpu.VMEM((2, 2, 56, T_CHILD), F32),
             pltpu.VMEM((2, 2, 128, T_CHILD), BF16),
             pltpu.VMEM((2, 2, 128, T_CHILD), BF16),
-            pltpu.VMEM((PARTS, 64, 16, LANES), F32),
-            pltpu.VMEM((PARTS, 64, 16, LANES), F32),
-            pltpu.VMEM((PARTS, 64, 16, LANES), F32),
-            pltpu.VMEM((PARTS, 64, 16, LANES), F32),
+            chunks, chunks, chunks, chunks,
+            groups,
             pltpu.VMEM((8, 2, 2, 2, 8, T_CHILD), F32),
-            pltpu.VMEM((8, 2, 2, 2, 8, T_CHILD), F32),
-            pltpu.VMEM((8, 2, 2, 2, 8, T_CHILD), F32),
+            pltpu.VMEM((16, 2, 8, T_CHILD), F32),
+            pltpu.VMEM((8, 2 * GROUP - 1, 2, 2, 2, T_CHILD), F32),
+            groups,
+            pltpu.VMEM((2, 2, 2, 56, T_CHILD), F32),
+            pltpu.VMEM((2, LANES, 256), F32),
+            pltpu.VMEM((2, 4, PARTS, 8, 8, LANES), F32),
             pltpu.VMEM((2, 8, PARTS, 8, 8, LANES), F32),
             pltpu.VMEM((8, 2, 8, 16 * LANES), F32),
             pltpu.VMEM((8, 2, 8, 16 * LANES), F32),
@@ -497,8 +648,9 @@
             pltpu.VMEM((2, 128, 8 * LANES), BF16),
             pltpu.VMEM((2, 128, 8 * LANES), BF16),
             pltpu.VMEM((2, 2, T_CHILD, LANES), F32),
-            pltpu.VMEM((2, 2, 2, 64, T_CHILD), F32),
-            pltpu.VMEM((2, 2, 64, T_CHILD), F32),
+            pltpu.VMEM((2, 2, 2, 56, T_CHILD), F32),
+            pltpu.VMEM((2, 2, 56, T_CHILD), F32),
+            pltpu.SemaphoreType.DMA((6,)),
             pltpu.SemaphoreType.DMA((4,)),
             pltpu.SemaphoreType.DMA((2,)),
             pltpu.SemaphoreType.DMA((2,)),
@@ -509,13 +661,12 @@
             pltpu.SemaphoreType.DMA((2,)),
         ],
         compiler_params=pltpu.CompilerParams(
-            collective_id=0, has_side_effects=True, vmem_limit_bytes=56 * 2**20),
+            collective_id=0, has_side_effects=True, vmem_limit_bytes=60 * 2**20),
         cost_estimate=pl.CostEstimate(flops=14_000_000_000, bytes_accessed=16_000_000, transcendentals=0),
         name="fields",
-    )(box_at_slot, octant, far_par, far_par_off, far_child, far_child_off, far_child_count,
-      x, t, tc, jnp.asarray(wide), jnp.asarray(narrow), jnp.asarray(phi_tables()), jnp.asarray(phi_angles()))
-    out = out.reshape(2, 2, 2, 8, 8, T_CHILD)[:, :, :, :, :GROUP].reshape(2, 2, 2, 56, T_CHILD)[:, :, :, :50]
-    return jnp.transpose(out, (3, 2, 1, 0, 4))
+    )(box_at_slot, octant, far_par.T, far_par_off.T, far_child.T, far_child_off.T, far_child_count,
+      child_rad, trans_par, trans_child,
+      jnp.asarray(wide), jnp.asarray(narrow), jnp.asarray(phi_tables()), jnp.asarray(phi_angles()))
 
 
 def solution(mesh):

time: 97.4 us -> 70.2 us (0.72)
  Pallas kernels: 81.1 us -> 67.9 us
  local copies, waits for them, and re-layouts: 15 us -> 2.11 us
  other arithmetic: 0.98 us -> 0 us
    pallas_call x1, Pallas kernels: 81.1 us -> 67.9 us  [shards(): pl.pallas_call(kernel, out_shape=jax.ShapeDtypeStruct((50, 2, 2, 2, T_CHI...]
    unnamed x20 -> x1, local copies, waits for them, and re-layouts: 7.35 us -> 2.11 us
    dynamic_slice x2 -> x0, local copies, waits for them, and re-layouts: 2.43 us -> none  [the longest x1 2.34 us: shards(): lax.dynamic_slice_in_dim(trans_par, 96 * b, 96, 3)]
    slice x2 -> x0, local copies, waits for them, and re-layouts: 1.68 us -> none  [the longest x1 1.67 us: shards(): out.reshape(2, 2, 2, 8, 8, T_CHILD)[:, :, :, :, :GROUP]]
    pad x2 -> x0, local copies, waits for them, and re-layouts: 1.36 us -> none  [the longest x1 1.14 us: shards(): jnp.pad(t, ((0, 0),) * 5 + ((0, LANES - 100),))]
    reshape x2 -> x0, local copies, waits for them, and re-layouts: 1.11 us -> none  [the longest x1 0.95 us: shards(): jnp.pad(x, ((0, 0),) * 4 + ((0, 1), (0, 0))).reshape(2, 2, 2, 64, T_CHILD)]
    transpose x1 -> x0, local copies, waits for them, and re-layouts: 1.03 us -> none  [shards(): return jnp.transpose(out, (3, 2, 1, 0, 4))]
    transpose x1 -> x0, other arithmetic: 0.98 us -> none  [shards(): tc = jnp.transpose(tc, (1, 2, 0, 3))]
where the time goes in v2:
time: 70.2 us; the launch traced here: 70 us
  Pallas kernels  67.9 us (97%)
  local copies, waits for them, and re-layouts  2.11 us (3%)
    pallas_call x1, Pallas kernels, shards(): pl.pallas_call(kernel, out_shape=jax.ShapeDtypeStruct((50, 2, 2, 2, T_CHI...  67.9 us
    unnamed x1, local copies, waits for them, and re-layouts  2.11 us

profile of v2, /device:TPU:1, one launch (start us, length us, event | category | flops | bytes accessed | tf_op | source)
XLA Modules:
  0.0 70.0 jit_solution(12740697392173031740)
XLA Ops:
  0.0 67.9 %fields.1 = f32[50,2,2,2,384]{4,3,2,1,0:T(2,128)} custom-call(s32[8]{0:T(128)} %bas.1, s32[16]{0:T(128)} %octant.1, s32[3,8]{1,0:T(4,128)} %bitcast.6, s32[3,8]{1,0:T(4,128)} %bitcast.7, s32[7,16]{1,0:T(8,128)} %bitcast.4, s32[7,16]{1,0:T(8,128)} %bitcast.5, s32[16]{0:T(128)} %far_count.1, f32[50,2,2,2,384]{4,3,2,1,0:T(2,128)} %x_hbm.1, ...), custom_call_target="tpu_custom_call" | custom-call | flops 14000000000 | bytes 16000000 | tf_op jit(solution)/shard_map/fields/pallas_call | solution.py:609
  67.9 2.1 %copy.16 = f32[50,2,2,2,384]{4,3,2,1,0:T(2,128)} copy(f32[50,2,2,2,384]{4,3,2,1,0:T(2,128)} %fields.1) | data formatting | bytes 1228800

commit v3 on v2

--- a/solution.py
+++ b/solution.py
@@ -43,9 +43,9 @@
     for kid in range(2):
         chip = 2 * pair + (place if kid == 0 else 1 - place)
         rows = table[(12 * chip + 4 * part + i).reshape(-1)]
-        wide.append(np.stack(split_np(rows)))
-        back = 0.25 * rows.reshape(PARTS, 256, T_CHILD).transpose(0, 2, 1)
-        narrow.append(np.stack(split_np(back)))
+        rows = rows.reshape(PARTS, 256, T_CHILD)
+        wide.append(np.concatenate(split_np(rows), axis=1))
+        narrow.append(np.concatenate(split_np(0.25 * rows.transpose(0, 2, 1)), axis=1))
     return np.stack(wide), np.stack(narrow)
 
 
@@ -71,7 +71,8 @@
                 at = np.ix_(rows, dd * LANES + np.arange(100))
                 plus[at] = 0.5 * (near + far)
                 minus[at] = 0.5 * (near - far)
-    return np.stack([np.stack(split_np(plus)), np.stack(split_np(minus))])
+    there = np.stack([np.stack(split_np(plus)), np.stack(split_np(minus))])
+    return there, np.ascontiguousarray(there.transpose(0, 1, 3, 2))
 
 
 @functools.cache
@@ -86,22 +87,24 @@
     return high, (x - high.astype(F32)).astype(BF16)
 
 
-NT = (((1,), (1,)), ((), ()))
-NN = (((1,), (0,)), ((), ()))
-
-
-def mul(a, b, dims):
-    return lax.dot_general(a, b, dims, preferred_element_type=F32)
+def mul(a, b):
+    return jnp.dot(a, b, preferred_element_type=F32)
+
+
+def mul_rows(both, w_high, w_low):
+    n = both.shape[0] // 2
+    got = mul(both, w_high)
+    return got[:n] + got[n:] + mul(both[:n], w_low)
 
 
 def kernel(
     bas, octant, far_par, far_par_off, far_child, far_child_off, far_count,
-    x_hbm, tab_hbm, tabc_hbm, wide_hbm, narrow_hbm, weights_hbm, angles,
+    x_hbm, tab_hbm, tabc_hbm, wide_hbm, narrow_hbm, weights_hbm, back_hbm, angles,
     out,
     slot_of, oct_lo, oct_hi, par_src, par_off, kid_src, kid_kid, kid_off, kid_act,
-    x_raw, tab_raw, tabc_raw, wide, narrow, weights,
+    x_raw, tab_raw, tabc_raw, wide, narrow, weights, weights_back,
     xf, x_swap, x_hi, x_lo, send1, recv1, send2, recv2,
-    child_recv, child, tabc, far_out, far_recv, far, tv, tab_send, tab_recv, tab, etab, y, pr, r_hi, r_lo, acc, own,
+    child_recv, child, tabc, far_out, far_recv, far, tv, tab_send, tab_recv, tab, etab, y, pr, r, acc, own,
     res_recv,
     s_in, s_swap, s_child, s_far, s_tab, s_tabf, s_main, s_back, s_loc,
 ):
@@ -132,6 +135,7 @@
         pltpu.make_async_copy(tabc_hbm.at[pl.ds(group, GROUP)], tabc_raw, s_in.at[3]),
         pltpu.make_async_copy(weights_hbm, weights, s_in.at[4]),
         pltpu.make_async_copy(narrow_hbm, narrow, s_in.at[5]),
+        pltpu.make_async_copy(back_hbm, weights_back, s_in.at[6]),
     ]
     loads[0].start()
     lax.fori_loop(1, 64, greet, 0)
@@ -163,10 +167,14 @@
         return carry
 
     loads[0].wait()
-    for p in range(2):
+
+    def phi_rows(p):
         for c in range(2):
             for k in range(2):
                 xf[p, c, k, 0:50, :] = x_raw[:, k, c, p, :]
+
+    for p in range(2):
+        pl.when(core != p)(functools.partial(phi_rows, p))
 
     pl.semaphore_wait(barrier, 64)
 
@@ -186,7 +194,8 @@
     child_own = pltpu.make_async_copy(x_raw.at[pl.ds(group, GROUP)], child_recv.at[b], s_loc.at[0])
     child_own.start()
 
-    lax.fori_loop(0, 16, kid_entry, 0)
+    for p in range(2):
+        pl.when(core == p)(functools.partial(phi_rows, p))
 
     lower = lax.broadcasted_iota(jnp.int32, (8, LANES), 0) < 4
     lane = lax.broadcasted_iota(jnp.int32, (8, LANES), 1)
@@ -205,40 +214,46 @@
     loads[2].wait()
     tv[...] = jnp.zeros_like(tv)
 
-    def tab_prepare(off, carry):
+    def tab_prepare(off):
         got = []
         for c in range(2):
             tv[c, 0:100, :] = tab_raw[:, off, c, :]
-            high, low = split(tv[c])
-            got.append((mul(picks[c], high, NT) + mul(picks[c], low, NT)).reshape(2, 3, 2, 2, 4, LANES))
+            high, low = split(jnp.transpose(tv[c]))
+            got.append(mul(picks[c], high) + mul(picks[c], low))
         flat = [g.reshape(12, 8, LANES) for g in got]
         even = jnp.where(lower[None], flat[0], flat[1]).reshape(2, 3, 2, 8, LANES)
         odd = jnp.where(lower[None], flat[1], flat[0]).reshape(2, 3, 2, 8, LANES)
         for s in range(2):
             for u in range(2):
-                tab_send[s, 2 * u, :, off] = even[s, :, u]
-                tab_send[s, 2 * u + 1, :, off] = odd[s, :, u]
-        return carry
-
-    lax.fori_loop(0, 8, tab_prepare, 0)
-
-    def tab_start(x, carry):
-        def go(s):
-            box = b if s == 0 else other_box
-            half = y_hi if s == 0 else 1 - y_hi
-            pltpu.make_async_remote_copy(
-                src_ref=tab_send.at[s, x], dst_ref=tab_recv.at[core, j], send_sem=s_tab.at[0], recv_sem=s_tab.at[1],
-                device_id=(box, (half * 4 + x) * 2 + core), device_id_type=MESH).start()
-
-        go(1)
-
-        @pl.when(x != x_at)
-        def _():
-            go(0)
-
-        return carry
-
-    lax.fori_loop(0, 4, tab_start, 0)
+                tab_send[s, 2 * u, off] = even[s, :, u]
+                tab_send[s, 2 * u + 1, off] = odd[s, :, u]
+
+    def tab_pair(pair, carry):
+        tab_prepare(2 * pair)
+        tab_prepare(2 * pair + 1)
+        at = pl.ds(2 * pair, 2)
+
+        def tab_start(x, carry):
+            def go(s):
+                box = b if s == 0 else other_box
+                half = y_hi if s == 0 else 1 - y_hi
+                pltpu.make_async_remote_copy(
+                    src_ref=tab_send.at[s, x, at], dst_ref=tab_recv.at[core, j, at],
+                    send_sem=s_tab.at[0], recv_sem=s_tab.at[1],
+                    device_id=(box, (half * 4 + x) * 2 + core), device_id_type=MESH).start()
+
+            go(1)
+
+            @pl.when(x != x_at)
+            def _():
+                go(0)
+
+            return carry
+
+        lax.fori_loop(0, 4, tab_start, 0)
+        return carry
+
+    lax.fori_loop(0, 4, tab_pair, 0)
     tab_recv[core, j] = tab_send[0, x_at]
 
     swap.wait()
@@ -249,7 +264,7 @@
             zero = core == 0
             full = jnp.concatenate(
                 [jnp.where(zero, mine, other), jnp.where(zero, other, mine), jnp.zeros((28, T_CHILD), F32)], axis=0)
-            high, low = split(full)
+            high, low = split(jnp.transpose(full))
             x_hi[c, k] = high
             x_lo[c, k] = low
         return carry
@@ -285,13 +300,11 @@
         return jnp.where(((lane >= 25 * m) & (lane < 25 * m + 25))[None], moved, extra)
 
     def widen(part, carry):
-        rows = pl.ds(pl.multiple_of(part * 256, 256), 256)
         for c in range(2):
             got = []
             for k in range(2):
-                hi, lo = x_hi[c, k], x_lo[c, k]
-                th, tl = wide[k, 0, rows, :], wide[k, 1, rows, :]
-                got.append(mul(th, hi, NT) + mul(th, lo, NT) + mul(tl, hi, NT))
+                both = mul(wide[k, part], x_hi[c, k])
+                got.append(both[:256] + both[256:] + mul(wide[k, part, 0:256, :], x_lo[c, k]))
             k0 = got[0].reshape(32, 8, LANES)
             k1 = got[1].reshape(32, 8, LANES)
             m = lower[None]
@@ -320,6 +333,7 @@
     lax.fori_loop(0, 2, send_forward, 0)
     send_all(2, 8, send1, recv1, s_main)
 
+    lax.fori_loop(0, 16, kid_entry, 0)
     loads[3].wait()
     for off in range(16):
         for c in range(2):
@@ -376,6 +390,7 @@
         device_id=buddy, device_id_type=MESH)
     tab_on.start()
     loads[4].wait()
+    loads[6].wait()
     tab_on.wait()
 
     row = lax.broadcasted_iota(jnp.int32, (8, LANES), 0)
@@ -405,7 +420,7 @@
                 etab[3 - o, 1, :, at] = -sin
             dcore, dj = lax.rem(blk, 2), blk // 2
             for off in range(8):
-                v = tab_recv[dcore, dj, part, off]
+                v = tab_recv[dcore, dj, off, part]
                 w = pltpu.roll(v, 4, 0)
                 one = jnp.where(lower, v, w)
                 two = jnp.where(lower, w, v)
@@ -439,11 +454,11 @@
             for jj in range(4):
                 one, two = got[:, jj], got[:, jj + 4]
                 pieces.append((one + two if sign == 0 else one - two).reshape(128, LANES))
-            high, low = split(jnp.concatenate(pieces, axis=1))
+            both = jnp.concatenate(split(jnp.concatenate(pieces, axis=1)), axis=0)
             for n in range(4):
                 cols = slice(n * 256, n * 256 + 256)
                 wh, wl = weights[sign, 0, :, cols], weights[sign, 1, :, cols]
-                y[sign, :, cols] = mul(high, wh, NN) + mul(low, wh, NN) + mul(high, wl, NN)
+                y[sign, :, cols] = mul_rows(both, wh, wl)
 
         def block(dd, carry):
             for half in range(2):
@@ -478,25 +493,23 @@
                 at_y = pl.ds(pl.multiple_of(dd * LANES, LANES), LANES)
                 for sign in range(2):
                     high, low = split(back[0] + back[1] if sign == 0 else back[0] - back[1])
-                    r_hi[sign, s * 16:s * 16 + 16, at_y] = high
-                    r_lo[sign, s * 16:s * 16 + 16, at_y] = low
+                    r[sign, s * 16:s * 16 + 16, at_y] = high
+                    r[sign, 128 + s * 16:144 + s * 16, at_y] = low
             return carry
 
         lax.fori_loop(0, 8, block, 0)
 
-        z = []
-        for sign in range(2):
-            high, low = r_hi[sign], r_lo[sign]
-            wh, wl = weights[sign, 0], weights[sign, 1]
-            z.append(mul(high, wh, NT) + mul(low, wh, NT) + mul(high, wl, NT))
-        one, two = z[0] + z[1], z[0] - z[1]
-        for jj in range(4):
-            cols = slice(jj * LANES, jj * LANES + LANES)
-            a = one[:, cols].reshape(8, 16, LANES)
-            c = two[:, cols].reshape(8, 16, LANES)
-            for s in range(8):
-                send2[part, s * 8 + jj] = a[s]
-                send2[part, s * 8 + jj + 4] = c[s]
+        for n in range(2):
+            cols = slice(n * 256, n * 256 + 256)
+            z = [mul_rows(r[sign], weights_back[sign, 0, :, cols], weights_back[sign, 1, :, cols])
+                 for sign in range(2)]
+            one, two = z[0] + z[1], z[0] - z[1]
+            for h in range(2):
+                a = one[:, h * LANES:h * LANES + LANES].reshape(8, 16, LANES)
+                c = two[:, h * LANES:h * LANES + LANES].reshape(8, 16, LANES)
+                for s in range(8):
+                    send2[part, s * 8 + 2 * n + h] = a[s]
+                    send2[part, s * 8 + 2 * n + h + 4] = c[s]
 
         for at_part in range(PARTS):
             @pl.when(part == at_part)
@@ -538,8 +551,8 @@
         for k in range(2):
             rows = jnp.where(m, even, odd) if k == 0 else jnp.where(m, odd, even)
             high, low = split(rows.reshape(256, LANES))
-            nh, nl = narrow[k, 0, part], narrow[k, 1, part]
-            acc[c, k] = acc[c, k] + (mul(nh, high, NN) + mul(nh, low, NN) + mul(nl, high, NN))
+            both = mul(narrow[k, part], high)
+            acc[c, k] = acc[c, k] + (both[:T_CHILD] + both[T_CHILD:] + mul(narrow[k, part, 0:T_CHILD, :], low))
 
     wait_all(0, 8, recv2, s_back.at[1, 0])
     narrow_tile(0, 0)
@@ -606,10 +619,11 @@
     anywhere = pl.BlockSpec(memory_space=pl.ANY)
     chunks = pltpu.VMEM((PARTS, 64, 16, LANES), F32)
     groups = pltpu.VMEM((8, GROUP, 2, 2, 2, T_CHILD), F32)
-    return pl.pallas_call(
+    there, back = phi_tables()
+    out = pl.pallas_call(
         kernel,
         out_shape=jax.ShapeDtypeStruct((50, 2, 2, 2, T_CHILD), F32),
-        in_specs=[smem] * 7 + [anywhere] * 6 + [vmem],
+        in_specs=[smem] * 7 + [anywhere] * 7 + [vmem],
         out_specs=vmem,
         scratch_shapes=[
             pltpu.SMEM((8,), jnp.int32),
@@ -626,11 +640,12 @@
             pltpu.VMEM((GROUP, 16, 2, T_CHILD), F32),
             pltpu.VMEM(wide.shape, BF16),
             pltpu.VMEM(narrow.shape, BF16),
-            pltpu.VMEM((2, 2, 4 * LANES, 8 * LANES), BF16),
+            pltpu.VMEM(there.shape, BF16),
+            pltpu.VMEM(back.shape, BF16),
             pltpu.VMEM((2, 2, 2, 56, T_CHILD), F32),
             pltpu.VMEM((2, 2, 56, T_CHILD), F32),
-            pltpu.VMEM((2, 2, 128, T_CHILD), BF16),
-            pltpu.VMEM((2, 2, 128, T_CHILD), BF16),
+            pltpu.VMEM((2, 2, T_CHILD, LANES), BF16),
+            pltpu.VMEM((2, 2, T_CHILD, LANES), BF16),
             chunks, chunks, chunks, chunks,
             groups,
             pltpu.VMEM((8, 2, 2, 2, 8, T_CHILD), F32),
@@ -639,18 +654,17 @@
             groups,
             pltpu.VMEM((2, 2, 2, 56, T_CHILD), F32),
             pltpu.VMEM((2, LANES, 256), F32),
-            pltpu.VMEM((2, 4, PARTS, 8, 8, LANES), F32),
-            pltpu.VMEM((2, 8, PARTS, 8, 8, LANES), F32),
+            pltpu.VMEM((2, 4, 8, PARTS, 8, LANES), F32),
+            pltpu.VMEM((2, 8, 8, PARTS, 8, LANES), F32),
             pltpu.VMEM((8, 2, 8, 16 * LANES), F32),
             pltpu.VMEM((8, 2, 8, 16 * LANES), F32),
             pltpu.VMEM((2, 128, 8 * LANES), F32),
             pltpu.VMEM((2, 8, 2, 8, LANES), F32),
-            pltpu.VMEM((2, 128, 8 * LANES), BF16),
-            pltpu.VMEM((2, 128, 8 * LANES), BF16),
+            pltpu.VMEM((2, 256, 8 * LANES), BF16),
             pltpu.VMEM((2, 2, T_CHILD, LANES), F32),
             pltpu.VMEM((2, 2, 2, 56, T_CHILD), F32),
             pltpu.VMEM((2, 2, 56, T_CHILD), F32),
-            pltpu.SemaphoreType.DMA((6,)),
+            pltpu.SemaphoreType.DMA((7,)),
             pltpu.SemaphoreType.DMA((4,)),
             pltpu.SemaphoreType.DMA((2,)),
             pltpu.SemaphoreType.DMA((2,)),
@@ -666,7 +680,8 @@
         name="fields",
     )(box_at_slot, octant, far_par.T, far_par_off.T, far_child.T, far_child_off.T, far_child_count,
       child_rad, trans_par, trans_child,
-      jnp.asarray(wide), jnp.asarray(narrow), jnp.asarray(phi_tables()), jnp.asarray(phi_angles()))
+      jnp.asarray(wide), jnp.asarray(narrow), jnp.asarray(there), jnp.asarray(back), jnp.asarray(phi_angles()))
+    return out
 
 
 def solution(mesh):

time: 70.2 us -> 65.4 us (0.932)
  Pallas kernels: 67.9 us -> 63 us
    pallas_call x1, Pallas kernels: 67.9 us -> 63 us  [shards(): pl.pallas_call(kernel, out_shape=jax.ShapeDtypeStruct((50, 2, 2, 2, T_CHI...]
where the time goes in v3:
time: 65.4 us; the launch traced here: 65.2 us
  Pallas kernels  63 us (96%)
  local copies, waits for them, and re-layouts  2.11 us (3%)
    pallas_call x1, Pallas kernels, shards(): pl.pallas_call(kernel, out_shape=jax.ShapeDtypeStruct((50, 2, 2, 2, T_CHI...  63 us
    unnamed x1, local copies, waits for them, and re-layouts  2.11 us

profile of v3, /device:TPU:1, one launch (start us, length us, event | category | flops | bytes accessed | tf_op | source)
XLA Modules:
  0.0 65.2 jit_solution(947811178634203172)
XLA Ops:
  0.0 63.0 %fields.1 = f32[50,2,2,2,384]{4,3,2,1,0:T(2,128)} custom-call(s32[8]{0:T(128)} %bas.1, s32[16]{0:T(128)} %octant.1, s32[3,8]{1,0:T(4,128)} %bitcast.6, s32[3,8]{1,0:T(4,128)} %bitcast.7, s32[7,16]{1,0:T(8,128)} %bitcast.4, s32[7,16]{1,0:T(8,128)} %bitcast.5, s32[16]{0:T(128)} %far_count.1, f32[50,2,2,2,384]{4,3,2,1,0:T(2,128)} %x_hbm.1, ...), custom_call_target="tpu_custom_call" | custom-call | flops 14000000000 | bytes 16000000 | tf_op jit(solution)/shard_map/fields/pallas_call | solution.py:623
  63.0 2.1 %copy.17 = f32[50,2,2,2,384]{4,3,2,1,0:T(2,128)} copy(f32[50,2,2,2,384]{4,3,2,1,0:T(2,128)} %fields.1) | data formatting | bytes 1228800

commit v4 on v3

--- a/solution.py
+++ b/solution.py
@@ -383,24 +383,14 @@
     far_own = pltpu.make_async_copy(far_out.at[b, pl.ds(far_row, GROUP)], far_recv.at[b], s_loc.at[1])
     far_own.start()
 
-    span = tab_recv.at[core, pl.ds(0, 7)]
-    pltpu.make_async_copy(span, span, s_tab.at[1]).wait()
-    tab_on = pltpu.make_async_remote_copy(
-        src_ref=tab_recv.at[core], dst_ref=tab_recv.at[core], send_sem=s_tabf.at[0], recv_sem=s_tabf.at[1],
-        device_id=buddy, device_id_type=MESH)
-    tab_on.start()
-    loads[4].wait()
-    loads[6].wait()
-    tab_on.wait()
-
     row = lax.broadcasted_iota(jnp.int32, (8, LANES), 0)
 
-    def one_part(part, carry):
+    def shift_tables(part, carry):
         q = (12 * me + 4 * part + lax.rem(row, 4)).astype(F32)
         theta = (q + 0.5) * (math.pi / T_PARENT)
         st, ct = 16.0 * jnp.sin(theta), 16.0 * jnp.cos(theta)
 
-        def prepare(blk, carry):
+        def shifts(blk, carry):
             at = pl.ds(pl.multiple_of(blk * LANES, LANES), LANES)
             ux, uy = st * angles[0, :, at], st * angles[1, :, at]
             for o in range(4):
@@ -414,10 +404,30 @@
                     0.235330630358893 + a * (-0.0258068913900141 + a * (0.00192957430940392
                     - a * 0.000104638104924846))))))
                 cos, sin = 1.0 - 2.0 * (s * s), 2.0 * (s * c)
-                etab[4 + o, 0, :, at] = cos
-                etab[4 + o, 1, :, at] = sin
-                etab[3 - o, 0, :, at] = cos
-                etab[3 - o, 1, :, at] = -sin
+                etab[part, 4 + o, 0, :, at] = cos
+                etab[part, 4 + o, 1, :, at] = sin
+                etab[part, 3 - o, 0, :, at] = cos
+                etab[part, 3 - o, 1, :, at] = -sin
+            return carry
+
+        lax.fori_loop(0, 16, shifts, 0)
+        return carry
+
+    lax.fori_loop(0, PARTS, shift_tables, 0)
+
+    span = tab_recv.at[core, pl.ds(0, 7)]
+    pltpu.make_async_copy(span, span, s_tab.at[1]).wait()
+    tab_on = pltpu.make_async_remote_copy(
+        src_ref=tab_recv.at[core], dst_ref=tab_recv.at[core], send_sem=s_tabf.at[0], recv_sem=s_tabf.at[1],
+        device_id=buddy, device_id_type=MESH)
+    tab_on.start()
+    loads[4].wait()
+    loads[6].wait()
+    tab_on.wait()
+
+    def one_part(part, carry):
+        def prepare(blk, carry):
+            at = pl.ds(pl.multiple_of(blk * LANES, LANES), LANES)
             dcore, dj = lax.rem(blk, 2), blk // 2
             for off in range(8):
                 v = tab_recv[dcore, dj, off, part]
@@ -469,8 +479,8 @@
                     ym = y[1, s * 16:s * 16 + 16, at_y]
                     v = yp + ym if half == 0 else yp - ym
                     vr, vi = v[:8], v[8:]
-                    cos = jnp.where(lower, etab[oct_lo[s], 0, :, at], etab[oct_hi[s], 0, :, at])
-                    sin = jnp.where(lower, etab[oct_lo[s], 1, :, at], etab[oct_hi[s], 1, :, at])
+                    cos = jnp.where(lower, etab[part, oct_lo[s], 0, :, at], etab[part, oct_hi[s], 0, :, at])
+                    sin = jnp.where(lower, etab[part, oct_lo[s], 1, :, at], etab[part, oct_hi[s], 1, :, at])
                     re = cos * vr - sin * vi
                     im = sin * vr + cos * vi
                     pr[half, s, 0] = re + pltpu.roll(re, 4, 0)
@@ -487,8 +497,8 @@
                         gr, gi = tr * fr - ti * fi, tr * fi + ti * fr
                         re = gr if re is None else re + gr
                         im = gi if im is None else im + gi
-                    cos = jnp.where(lower, etab[oct_lo[s], 0, :, at], etab[oct_hi[s], 0, :, at])
-                    sin = jnp.where(lower, etab[oct_lo[s], 1, :, at], etab[oct_hi[s], 1, :, at])
+                    cos = jnp.where(lower, etab[part, oct_lo[s], 0, :, at], etab[part, oct_hi[s], 0, :, at])
+                    sin = jnp.where(lower, etab[part, oct_lo[s], 1, :, at], etab[part, oct_hi[s], 1, :, at])
                     back.append(jnp.concatenate([cos * re + sin * im, cos * im - sin * re], axis=0))
                 at_y = pl.ds(pl.multiple_of(dd * LANES, LANES), LANES)
                 for sign in range(2):
@@ -557,13 +567,39 @@
     wait_all(0, 8, recv2, s_back.at[1, 0])
     narrow_tile(0, 0)
 
-    def narrow_part(part, carry):
-        wait_all(part, 16, recv2, s_back.at[1, part])
-        for c in range(2):
-            narrow_tile(part, c)
-        return carry
-
-    lax.fori_loop(1, PARTS, narrow_part, 0)
+    def hand_over(c):
+        return pltpu.make_async_remote_copy(
+            src_ref=own.at[1 - core, c], dst_ref=res_recv.at[c], send_sem=s_swap.at[2 + c], recv_sem=s_swap.at[4 + c],
+            device_id=buddy, device_id_type=MESH)
+
+    def finish(c):
+        for k in range(2):
+            full = jnp.transpose(acc[c, k])
+            own[0, c, k, 0:50, :] = full[0:50]
+            own[1, c, k, 0:50, :] = full[50:100]
+        hand_over(c).start()
+
+    def keep(c):
+        for p in range(2):
+            @pl.when(core == p)
+            def _():
+                for k in range(2):
+                    out[:, k, c, p, :] = own[p, c, k, 0:50, :] + far[p, c, k, 0:50, :]
+
+    def take_over(c):
+        hand_over(c).wait()
+        for p in range(2):
+            @pl.when(core != p)
+            def _():
+                for k in range(2):
+                    out[:, k, c, p, :] = res_recv[c, k, 0:50, :] + far[p, c, k, 0:50, :]
+
+    wait_all(1, 16, recv2, s_back.at[1, 1])
+    narrow_tile(1, 0)
+    narrow_tile(1, 1)
+    wait_all(2, 16, recv2, s_back.at[1, 2])
+    narrow_tile(2, 0)
+    finish(0)
 
     def take_back(i, carry):
         at = pl.ds(i * 8, 8)
@@ -574,31 +610,13 @@
         return carry
 
     lax.fori_loop(0, 8, take_back, 0)
+    narrow_tile(2, 1)
     narrow_tile(0, 1)
-
-    for c in range(2):
-        for k in range(2):
-            full = jnp.transpose(acc[c, k])
-            own[0, c, k, 0:50, :] = full[0:50]
-            own[1, c, k, 0:50, :] = full[50:100]
-    swap2 = pltpu.make_async_remote_copy(
-        src_ref=own.at[1 - core], dst_ref=res_recv, send_sem=s_swap.at[2], recv_sem=s_swap.at[3],
-        device_id=buddy, device_id_type=MESH)
-    swap2.start()
-    for p in range(2):
-        @pl.when(core == p)
-        def _():
-            for c in range(2):
-                for k in range(2):
-                    out[:, k, c, p, :] = own[p, c, k, 0:50, :] + far[p, c, k, 0:50, :]
-
-    swap2.wait()
-    for p in range(2):
-        @pl.when(core != p)
-        def _():
-            for c in range(2):
-                for k in range(2):
-                    out[:, k, c, p, :] = res_recv[c, k, 0:50, :] + far[p, c, k, 0:50, :]
+    finish(1)
+    keep(0)
+    keep(1)
+    take_over(0)
+    take_over(1)
 
     for part in range(PARTS):
         wait_all(part, 8 if part == 2 else 16, send1, s_main.at[0, part])
@@ -622,7 +640,7 @@
     there, back = phi_tables()
     out = pl.pallas_call(
         kernel,
-        out_shape=jax.ShapeDtypeStruct((50, 2, 2, 2, T_CHILD), F32),
+        out_shape=pltpu.VMEM((50, 2, 2, 2, T_CHILD), F32),
         in_specs=[smem] * 7 + [anywhere] * 7 + [vmem],
         out_specs=vmem,
         scratch_shapes=[
@@ -657,7 +675,7 @@
             pltpu.VMEM((2, 4, 8, PARTS, 8, LANES), F32),
             pltpu.VMEM((2, 8, 8, PARTS, 8, LANES), F32),
             pltpu.VMEM((8, 2, 8, 16 * LANES), F32),
-            pltpu.VMEM((8, 2, 8, 16 * LANES), F32),
+            pltpu.VMEM((PARTS, 8, 2, 8, 16 * LANES), F32),
             pltpu.VMEM((2, 128, 8 * LANES), F32),
             pltpu.VMEM((2, 8, 2, 8, LANES), F32),
             pltpu.VMEM((2, 256, 8 * LANES), BF16),
@@ -665,7 +683,7 @@
             pltpu.VMEM((2, 2, 2, 56, T_CHILD), F32),
             pltpu.VMEM((2, 2, 56, T_CHILD), F32),
             pltpu.SemaphoreType.DMA((7,)),
-            pltpu.SemaphoreType.DMA((4,)),
+            pltpu.SemaphoreType.DMA((6,)),
             pltpu.SemaphoreType.DMA((2,)),
             pltpu.SemaphoreType.DMA((2,)),
             pltpu.SemaphoreType.DMA((2,)),

time: 65.4 us -> 62.5 us (0.956)
  Pallas kernels: 63 us -> 61.5 us
  local copies, waits for them, and re-layouts: 2.11 us -> 0.83 us
    pallas_call x1, Pallas kernels: 63 us -> 61.5 us  [shards(): pl.pallas_call(kernel, out_shape=pltpu.VMEM((50, 2, 2, 2, T_CHILD), F32),...]
    unnamed x1, local copies, waits for them, and re-layouts: 2.11 us -> 0.83 us
where the time goes in v4:
time: 62.5 us; the launch traced here: 62.3 us
  Pallas kernels  61.5 us (98%)
  local copies, waits for them, and re-layouts  0.83 us (1%)
    pallas_call x1, Pallas kernels, shards(): pl.pallas_call(kernel, out_shape=pltpu.VMEM((50, 2, 2, 2, T_CHILD), F32),...  61.5 us

profile of v4, /device:TPU:1, one launch (start us, length us, event | category | flops | bytes accessed | tf_op | source)
XLA Modules:
  0.0 62.3 jit_solution(5811310429996607065)
XLA Ops:
  0.0 61.5 %fields.1 = f32[50,2,2,2,384]{4,3,2,1,0:T(2,128)S(1)} custom-call(s32[8]{0:T(128)} %bas.1, s32[16]{0:T(128)} %octant.1, s32[3,8]{1,0:T(4,128)} %bitcast.6, s32[3,8]{1,0:T(4,128)} %bitcast.7, s32[7,16]{1,0:T(8,128)} %bitcast.4, s32[7,16]{1,0:T(8,128)} %bitcast.5, s32[16]{0:T(128)} %far_count.1, f32[50,2,2,2,384]{4,3,2,1,0:T(2,128)} %x_hbm.1, ...), custom_call_target="tpu_custom_call" | custom-call | flops 14000000000 | bytes 16000000 | tf_op jit(solution)/shard_map/fields/pallas_call | solution.py:641
  61.5 0.8 %copy.17 = f32[50,2,2,2,384]{4,3,2,1,0:T(2,128)} copy(f32[50,2,2,2,384]{4,3,2,1,0:T(2,128)S(1)} %fields.1) | data formatting | bytes 1228800

commit v5 on v4

--- a/solution.py
+++ b/solution.py
@@ -126,7 +126,10 @@
         pl.semaphore_signal(barrier, inc=1, device_id=chip(lax.rem(me + i, 64)), device_id_type=MESH)
         return carry
 
-    group = jnp.minimum(GROUP * b, 50 - GROUP)
+    def group_of(g):
+        return 6 * g + jnp.maximum(g - 6, 0)
+
+    group = group_of(b)
     window = pl.multiple_of((3 * (b // 2)) // 2 * LANES, LANES)
     loads = [
         pltpu.make_async_copy(x_hbm, x_raw, s_in.at[0]),
@@ -185,10 +188,23 @@
 
     def child_start(i, carry):
         g = lax.rem(b + i, 8)
-        pltpu.make_async_remote_copy(
-            src_ref=x_raw.at[pl.ds(jnp.minimum(GROUP * g, 50 - GROUP), GROUP)], dst_ref=child_recv.at[b],
-            send_sem=s_child.at[0], recv_sem=s_child.at[1], device_id=(g, d), device_id_type=MESH).start()
-        return carry
+
+        def go(row, count, n):
+            pltpu.make_async_remote_copy(
+                src_ref=x_raw.at[pl.ds(group_of(g) + row, count)], dst_ref=child_recv.at[b, pl.ds(row, count)],
+                send_sem=s_child.at[0, n], recv_sem=s_child.at[1, n], device_id=(g, d), device_id_type=MESH).start()
+
+        go(0, 6, 0)
+
+        @pl.when(g >= 6)
+        def _():
+            go(6, 1, 1)
+
+        return carry
+
+    def wait_rows(ref, first, row, count, sem):
+        span = ref.at[pl.ds(0, first), pl.ds(row, count)]
+        pltpu.make_async_copy(span, span, sem).wait()
 
     lax.fori_loop(1, 8, child_start, 0)
     child_own = pltpu.make_async_copy(x_raw.at[pl.ds(group, GROUP)], child_recv.at[b], s_loc.at[0])
@@ -339,8 +355,12 @@
         for c in range(2):
             tabc[off, c, 0:GROUP, :] = tabc_raw[:, off, c, :]
     child_own.wait()
-    span = child_recv.at[pl.ds(0, 7)]
-    pltpu.make_async_copy(span, span, s_child.at[1]).wait()
+    wait_rows(child_recv, 7, 0, 6, s_child.at[1, 0])
+
+    @pl.when(b >= 6)
+    def _():
+        wait_rows(child_recv, 7, 6, 1, s_child.at[1, 1])
+
 
     def child_rows(src, carry):
         for p in range(2):
@@ -370,17 +390,24 @@
 
     lax.fori_loop(0, 8, far_slot, 0)
 
-    far_row = jnp.where(b == 7, GROUP - 1, 0)
-
     def far_start(i, carry):
         to = lax.rem(b + i, 8)
-        pltpu.make_async_remote_copy(
-            src_ref=far_out.at[to, pl.ds(far_row, GROUP)], dst_ref=far_recv.at[b],
-            send_sem=s_far.at[0], recv_sem=s_far.at[1], device_id=(to, d), device_id_type=MESH).start()
+
+        def go(row, count, n):
+            pltpu.make_async_remote_copy(
+                src_ref=far_out.at[to, pl.ds(row, count)], dst_ref=far_recv.at[b, pl.ds(row, count)],
+                send_sem=s_far.at[0, n], recv_sem=s_far.at[1, n], device_id=(to, d), device_id_type=MESH).start()
+
+        go(0, 6, 0)
+
+        @pl.when(b >= 6)
+        def _():
+            go(6, 1, 1)
+
         return carry
 
     lax.fori_loop(1, 8, far_start, 0)
-    far_own = pltpu.make_async_copy(far_out.at[b, pl.ds(far_row, GROUP)], far_recv.at[b], s_loc.at[1])
+    far_own = pltpu.make_async_copy(far_out.at[b], far_recv.at[b], s_loc.at[1])
     far_own.start()
 
     row = lax.broadcasted_iota(jnp.int32, (8, LANES), 0)
@@ -542,14 +569,22 @@
     lax.fori_loop(0, PARTS, one_part, 0)
 
     far_own.wait()
-    span = far_recv.at[pl.ds(0, 7)]
-    pltpu.make_async_copy(span, span, s_far.at[1]).wait()
+    wait_rows(far_recv, 7, 0, 6, s_far.at[1, 0])
+
+    @pl.when(b >= 6)
+    def _():
+        wait_rows(far_recv, 1, 6, 1, s_far.at[1, 1])
+
+    @pl.when(b < 6)
+    def _():
+        wait_rows(far_recv, 2, 6, 1, s_far.at[1, 1])
+
     for p in range(2):
         for c in range(2):
             for k in range(2):
                 for g in range(8):
-                    count = GROUP if g < 7 else 1
-                    far[p, c, k, g * GROUP:g * GROUP + count, :] = far_recv[g, 0:count, k, c, p, :]
+                    first, count = 6 * g + max(g - 6, 0), 6 + (g >= 6)
+                    far[p, c, k, first:first + count, :] = far_recv[g, 0:count, k, c, p, :]
 
     loads[5].wait()
     acc[...] = jnp.zeros_like(acc)
@@ -621,10 +656,18 @@
     for part in range(PARTS):
         wait_all(part, 8 if part == 2 else 16, send1, s_main.at[0, part])
         wait_all(part, 8 if part == 0 else 16, send2, s_back.at[0, part])
-    span = child_recv.at[pl.ds(0, 7)]
-    pltpu.make_async_copy(span, span, s_child.at[0]).wait()
-    span = far_recv.at[pl.ds(0, 7)]
-    pltpu.make_async_copy(span, span, s_far.at[0]).wait()
+    wait_rows(child_recv, 7, 0, 6, s_child.at[0, 0])
+    wait_rows(far_recv, 7, 0, 6, s_far.at[0, 0])
+
+    @pl.when(b >= 6)
+    def _():
+        wait_rows(child_recv, 1, 6, 1, s_child.at[0, 1])
+        wait_rows(far_recv, 7, 6, 1, s_far.at[0, 1])
+
+    @pl.when(b < 6)
+    def _():
+        wait_rows(child_recv, 2, 6, 1, s_child.at[0, 1])
+
     span = tab_recv.at[core, pl.ds(0, 7)]
     pltpu.make_async_copy(span, span, s_tab.at[0]).wait()
 
@@ -668,7 +711,7 @@
             groups,
             pltpu.VMEM((8, 2, 2, 2, 8, T_CHILD), F32),
             pltpu.VMEM((16, 2, 8, T_CHILD), F32),
-            pltpu.VMEM((8, 2 * GROUP - 1, 2, 2, 2, T_CHILD), F32),
+            groups,
             groups,
             pltpu.VMEM((2, 2, 2, 56, T_CHILD), F32),
             pltpu.VMEM((2, LANES, 256), F32),
@@ -684,8 +727,8 @@
             pltpu.VMEM((2, 2, 56, T_CHILD), F32),
             pltpu.SemaphoreType.DMA((7,)),
             pltpu.SemaphoreType.DMA((6,)),
-            pltpu.SemaphoreType.DMA((2,)),
-            pltpu.SemaphoreType.DMA((2,)),
+            pltpu.SemaphoreType.DMA((2, 2)),
+            pltpu.SemaphoreType.DMA((2, 2)),
             pltpu.SemaphoreType.DMA((2,)),
             pltpu.SemaphoreType.DMA((2,)),
             pltpu.SemaphoreType.DMA((2, PARTS)),

time: 62.5 us -> 61.7 us (0.987)
  Pallas kernels: 61.5 us -> 60.7 us
    pallas_call x1, Pallas kernels: 61.5 us -> 60.7 us  [shards(): pl.pallas_call(kernel, out_shape=pltpu.VMEM((50, 2, 2, 2, T_CHILD), F32),...]
where the time goes in v5:
time: 61.7 us; the launch traced here: 61.6 us
  Pallas kernels  60.7 us (98%)
  local copies, waits for them, and re-layouts  0.83 us (1%)
    pallas_call x1, Pallas kernels, shards(): pl.pallas_call(kernel, out_shape=pltpu.VMEM((50, 2, 2, 2, T_CHILD), F32),...  60.7 us

profile of v5, /device:TPU:1, one launch (start us, length us, event | category | flops | bytes accessed | tf_op | source)
XLA Modules:
  0.0 61.6 jit_solution(3930449258161905913)
XLA Ops:
  0.0 60.7 %fields.1 = f32[50,2,2,2,384]{4,3,2,1,0:T(2,128)S(1)} custom-call(s32[8]{0:T(128)} %bas.1, s32[16]{0:T(128)} %octant.1, s32[3,8]{1,0:T(4,128)} %bitcast.6, s32[3,8]{1,0:T(4,128)} %bitcast.7, s32[7,16]{1,0:T(8,128)} %bitcast.4, s32[7,16]{1,0:T(8,128)} %bitcast.5, s32[16]{0:T(128)} %far_count.1, f32[50,2,2,2,384]{4,3,2,1,0:T(2,128)} %x_hbm.1, ...), custom_call_target="tpu_custom_call" | custom-call | flops 14000000000 | bytes 16000000 | tf_op jit(solution)/shard_map/fields/pallas_call | solution.py:684
  60.8 0.8 %copy.17 = f32[50,2,2,2,384]{4,3,2,1,0:T(2,128)} copy(f32[50,2,2,2,384]{4,3,2,1,0:T(2,128)S(1)} %fields.1) | data formatting | bytes 1228800

commit v6 on v5

--- a/solution.py
+++ b/solution.py
@@ -632,19 +632,21 @@
     wait_all(1, 16, recv2, s_back.at[1, 1])
     narrow_tile(1, 0)
     narrow_tile(1, 1)
+
+    def take_back(part, i, carry):
+        at = pl.ds(i * 8, 8)
+        extra = jnp.zeros((8, 8, LANES), F32) if part == 1 else recv2[0, at, 8:16, :]
+        for h in range(2):
+            extra = unstow(2 * part - 2 + h, recv2[part, at, 8 * h:8 * h + 8, :], extra)
+        recv2[0, at, 8:16, :] = extra
+        return carry
+
+    lax.fori_loop(0, 8, functools.partial(take_back, 1), 0)
     wait_all(2, 16, recv2, s_back.at[1, 2])
     narrow_tile(2, 0)
     finish(0)
 
-    def take_back(i, carry):
-        at = pl.ds(i * 8, 8)
-        extra = jnp.zeros((8, 8, LANES), F32)
-        for m in range(4):
-            extra = unstow(m, recv2[1 + m // 2, at, 8 * (m % 2):8 * (m % 2) + 8, :], extra)
-        recv2[0, at, 8:16, :] = extra
-        return carry
-
-    lax.fori_loop(0, 8, take_back, 0)
+    lax.fori_loop(0, 8, functools.partial(take_back, 2), 0)
     narrow_tile(2, 1)
     narrow_tile(0, 1)
     finish(1)

time: 61.7 us -> 61.6 us (level)
  no operation moved by 1% of the time
where the time goes in v6:
time: 61.6 us; the launch traced here: 61.4 us
  Pallas kernels  60.6 us (98%)
  local copies, waits for them, and re-layouts  0.83 us (1%)
    pallas_call x1, Pallas kernels, shards(): pl.pallas_call(kernel, out_shape=pltpu.VMEM((50, 2, 2, 2, T_CHILD), F32),...  60.6 us

profile of v6, /device:TPU:1, one launch (start us, length us, event | category | flops | bytes accessed | tf_op | source)
XLA Modules:
  0.0 61.4 jit_solution(13004636688025863949)
XLA Ops:
  0.0 60.6 %fields.1 = f32[50,2,2,2,384]{4,3,2,1,0:T(2,128)S(1)} custom-call(s32[8]{0:T(128)} %bas.1, s32[16]{0:T(128)} %octant.1, s32[3,8]{1,0:T(4,128)} %bitcast.6, s32[3,8]{1,0:T(4,128)} %bitcast.7, s32[7,16]{1,0:T(8,128)} %bitcast.4, s32[7,16]{1,0:T(8,128)} %bitcast.5, s32[16]{0:T(128)} %far_count.1, f32[50,2,2,2,384]{4,3,2,1,0:T(2,128)} %x_hbm.1, ...), custom_call_target="tpu_custom_call" | custom-call | flops 14000000000 | bytes 16000000 | tf_op jit(solution)/shard_map/fields/pallas_call | solution.py:686
  60.6 0.8 %copy.17 = f32[50,2,2,2,384]{4,3,2,1,0:T(2,128)} copy(f32[50,2,2,2,384]{4,3,2,1,0:T(2,128)S(1)} %fields.1) | data formatting | bytes 1228800
